TPU v7x, 256 devices: a whole 4x4x8 slice. The times are simulated.
256 devices in a mesh: seq: 32 (over z_hi, y, core), head: 8 (over z_lo, x).
Axes of the slice: x: 4, y: 4, z: 8 (z_hi: 4, z_lo: 2; z = z_hi * 2 + z_lo), core: 2. Of those that a mesh axis runs over, the one named last changes fastest.
Arguments:
- queries: bfloat16 [16384, 2048], P('seq', 'head'), may hold values from -25 to 25
- key_frames: bfloat16 [16384, 2048], P('seq', 'head'), may hold values from -4 to 4
- value_frames: bfloat16 [16384, 2048], P('seq', 'head'), may hold values from -6 to 6
- out_weight: bfloat16 [2048, 2048], P('head'), may hold values from -0.125 to 0.125
- out_grad: bfloat16 [16384, 2048], P('seq', 'head'), may hold values from -6 to 6
- near_window: int32 [32], replicated, may hold values from 1 to 2, as said below
- mid_start: int32 [32], replicated, may hold values from 0 to 31, as said below
Outputs:
- layer_out: bfloat16 [16384, 2048], P('seq', 'head')
- query_grad: bfloat16 [16384, 2048], P('seq', 'head')
- key_grad: bfloat16 [16384, 2048], P('seq', 'head')
- value_grad: bfloat16 [16384, 2048], P('seq', 'head')
- weight_grad: float32 [2048, 2048], P('head', 'seq')
Inputs may be any that keep to these rules, and one draw needn't show every extreme that they name: mid_start[b] lies between 0 and b; the last block's value is 31. near_window is 1 on block 0 and 2 on every other block.
All inputs are finite; a program needn't handle non-finite values.
Results may differ from a plain program's by a relative error of at most 0.028.
Values may be sent and summed in bfloat16 or wider, within the bound.
No kernel may reach another device: no remote copies, remote signals or barrier semaphores. Data moves between devices by JAX's collectives and lax.ppermute only.
A program may use at most 128 MiB of HBM per device.

v0:
```python
import math

import jax
import jax.numpy as jnp
from jax import lax
from jax.experimental import pallas as pl
from jax.experimental.pallas import tpu as pltpu
from jax.sharding import PartitionSpec as P

HEAD_DIM = 128
BLOCK = 512
POOL_MID = 8
MIDS = BLOCK // POOL_MID
HEADS_DEV = 2
COLS = HEADS_DEV * HEAD_DIM
Z, Y, C = 4, 4, 2
ZL, X = 2, 4
CHUNK = Z * MIDS
CHUNKS = Y * C
FAR_KEYS = CHUNKS * CHUNK
HALF = BLOCK // 2
SUM_COLS = 3 * COLS

NEGATIVE = -1e30
SCALING = HEAD_DIM ** (-0.5)
SCORE_SCALE = SCALING * math.log2(math.e)
MID_BIAS = math.log2(POOL_MID)

bf16 = jnp.bfloat16
f32 = jnp.float32


def along_seq(value, dz=0, dy=0, dc=0):
    pairs = []
    for z in range(Z):
        for y in range(Y):
            for c in range(C):
                target = (((z + dz) % Z) * Y + (y + dy) % Y) * C + (c + dc) % C
                pairs.append(((z * Y + y) * C + c, target))
    return lax.ppermute(value, "seq", pairs)


def along_head(value, dz=0, dx=0):
    pairs = []
    for z in range(ZL):
        for x in range(X):
            pairs.append((z * X + x, ((z + dz) % ZL) * X + (x + dx) % X))
    return lax.ppermute(value, "head", pairs)


def along_z(value, step):
    return along_seq(value, dz=step)


def along_y(value, step):
    return along_seq(value, dy=step)


def along_x(value, step):
    return along_head(value, dx=step)


def passed_along(value, steps):
    count = Z * Y * C
    initial, last = (max(0, -steps), min(count, count - steps))
    return lax.ppermute(value, "seq", [(source, source + steps) for source in range(initial, last)])


def shape(*dims, dtype=bf16):
    return jax.ShapeDtypeStruct(dims, dtype)


def call(kernel, outs, scratch=(), far=0, flops=0, count=0, after=()):
    def run(*args):
        moved = sum(a.size * a.dtype.itemsize for a in (*args, *outs))

        def body(*refs):
            kernel(*refs[: len(args)], *refs[len(args) + len(after) :])

        return pl.pallas_call(
            body,
            out_shape=list(outs),
            in_specs=[pl.BlockSpec(memory_space=pl.ANY)] * far
            + [pl.BlockSpec(memory_space=pltpu.VMEM)] * (len(args) - far)
            + [pl.BlockSpec(memory_space=pl.ANY)] * len(after),
            out_specs=[pl.BlockSpec(memory_space=pltpu.VMEM)] * len(outs),
            scratch_shapes=list(scratch),
            cost_estimate=pl.CostEstimate(flops=flops, bytes_accessed=moved, transcendentals=count),
            compiler_params=pltpu.CompilerParams(vmem_limit_bytes=26 * 1024 * 1024),
        )(*args, *after)

    return run


def place():
    s = lax.axis_index("seq")
    return s, s >> 3, (s >> 1) & 3, s & 1


def block_of(z, y, c, group, dz):
    core = (c + (group >> 2)) & 1
    return ((z - dz) & 3) * 8 + ((y - group) & 3) * 2 + core


def dot(a, b, da, db):
    return lax.dot_general(a, b, (((da,), (db,)), ((), ())), preferred_element_type=f32)


def wide(ref, rows):
    return ref[rows].astype(f32)


def emit(chunk, outs):
    behind, ahead, late_behind, late_ahead, own = outs
    h = chunk(0).shape[0] // 2
    behind[:h], behind[h:] = chunk(1)[h:], chunk(2)[:h]
    ahead[:h], ahead[h:] = chunk(3)[:h], chunk(2)[h:]
    late_behind[...], late_ahead[...] = chunk(1)[:h], chunk(3)[h:]
    own[...] = chunk(0)


def ring_shapes(rows, width):
    h = rows // 2
    return [shape(rows, width)] * 2 + [shape(h, width)] * 2 + [shape(rows, width)]


def turn_kernel(late_behind, late_ahead, got_behind, got_ahead, out_behind, out_ahead):
    h = late_behind.shape[0]
    rest, all_rows = slice(h, 2 * h), slice(0, h)
    out_behind[...] = (wide(late_behind, all_rows) + wide(got_behind, rest)).astype(bf16)
    out_ahead[...] = (wide(late_ahead, all_rows) + wide(got_ahead, rest)).astype(bf16)


def ring(parts, along, after=()):
    behind, ahead, late_behind, late_ahead, own = parts
    got_behind, got_ahead = along(behind, -1), along(ahead, 1)
    turned = [shape(*late_behind.shape)] * 2
    out_behind, out_ahead = call(turn_kernel, turned, after=after)(
        late_behind, late_ahead, got_behind, got_ahead
    )
    return own, got_behind, got_ahead, along(out_behind, -1), along(out_ahead, 1)


def halves(own, got_behind, got_ahead, last_behind, last_ahead):
    h = last_behind.shape[0]
    first, rest = slice(0, h), slice(h, 2 * h)
    a = wide(own, first) + wide(got_ahead, first) + wide(last_behind, first)
    b = wide(own, rest) + wide(got_behind, first) + wide(last_ahead, first)
    return a, b


def pool_kernel(k_hbm, v_hbm, kv_ref, mid_ref, sems):
    copies = [
        pltpu.make_async_copy(k_hbm, kv_ref.at[:, :COLS], sems.at[0]),
        pltpu.make_async_copy(v_hbm, kv_ref.at[:, COLS:], sems.at[1]),
    ]
    for copy in copies:
        copy.start()
    row = lax.broadcasted_iota(jnp.int32, (MIDS, BLOCK), 0)
    col = lax.broadcasted_iota(jnp.int32, (MIDS, BLOCK), 1)
    mean = jnp.where(row == col // POOL_MID, 1.0 / POOL_MID, 0.0).astype(bf16)
    for copy in copies:
        copy.wait()
    mid_ref[...] = dot(mean, kv_ref[...], 1, 0).astype(bf16)


def gather_kernel(mid_ref, a, b, c, kv_ref, run_ref, kv_out):
    for i, ref in enumerate((mid_ref, a, b, c)):
        run_ref[i * MIDS : (i + 1) * MIDS] = ref[...]
    kv_out[...] = kv_ref[...]


def part_kernel(run_ref, ahead_ref, behind_ref, three_ref, first_ref, rest_ref):
    h = CHUNK // 2
    for i, ref in enumerate((run_ref, ahead_ref, behind_ref)):
        three_ref[i * CHUNK : (i + 1) * CHUNK] = ref[...]
    first_ref[...] = ahead_ref[:h]
    rest_ref[...] = behind_ref[h:]


def own_mask(first_key):
    key = lax.broadcasted_iota(jnp.int32, (HALF, BLOCK), 0) + first_key
    query = lax.broadcasted_iota(jnp.int32, (HALF, BLOCK), 1)
    return key <= query


def chunk_bias(bias_ref, g, scores):
    return jnp.concatenate(
        [scores[d * MIDS : (d + 1) * MIDS] + bias_ref[g * Z + d] for d in range(Z)], axis=0
    )


def chunk_rows(g):
    return pl.ds(pl.multiple_of(g * CHUNK, CHUNK), CHUNK)


def head_cols(h):
    return slice(h * HEAD_DIM, (h + 1) * HEAD_DIM), slice(
        COLS + h * HEAD_DIM, COLS + (h + 1) * HEAD_DIM
    )


def weight_cols(zl, x, dx, dz):
    device = ((zl + dz) & 1) * X + ((x - dx) & 3)
    return device, pl.ds(pl.multiple_of(device * COLS, COLS), COLS)


def forward_kernel(
    nw_hbm, ms_hbm, q_ref, w_ref, kv_ref, pkv_ref, *refs
):
    mids = []
    for three, first, rest in (refs[:3], refs[3:6]):
        runs = [three[i * CHUNK : (i + 1) * CHUNK] for i in range(3)]
        mids += [runs[0], runs[1], jnp.concatenate([first[...], rest[...]], axis=0), runs[2]]
    att_ref, lse_ref, far_ref, *outs = refs[6:14]
    s_ref, nw_ref, ms_ref, bias_ref, sems = refs[14:]
    copies = [
        pltpu.make_async_copy(a, b, sems.at[i])
        for i, (a, b) in enumerate(((nw_hbm, nw_ref), (ms_hbm, ms_ref)))
    ]
    for copy in copies:
        copy.start()
    s, z, y, c = place()
    row = lax.broadcasted_iota(jnp.int32, (CHUNK, CHUNK), 0)
    col = lax.broadcasted_iota(jnp.int32, (CHUNK, CHUNK), 1)
    same = jnp.where(row == col, 1.0, 0.0)
    mean = jnp.where(row // POOL_MID == col // POOL_MID, 1.0 / POOL_MID, 0.0)
    for copy in copies:
        copy.wait()
    near_begin = jnp.maximum(s + 1 - nw_ref[s], 0)
    mid_begin = jnp.minimum(ms_ref[s], near_begin)
    for g in range(CHUNKS):
        picks = []
        for dz in range(Z):
            b = block_of(z, y, c, g, dz)
            bias_ref[g * Z + dz] = jnp.where(b < near_begin, MID_BIAS, NEGATIVE)
            far = jnp.where(b < mid_begin, 1.0, 0.0)
            rows = slice(dz * MIDS, (dz + 1) * MIDS)
            picks.append(same[rows] + far * (mean[rows] - same[rows]))
        pick = jnp.concatenate(picks, axis=0).astype(bf16)
        far_ref[g * CHUNK : (g + 1) * CHUNK, :] = dot(pick, mids[g], 1, 0).astype(bf16)
    prev_bias = jnp.where(near_begin < s, 0.0, NEGATIVE)
    for h in range(HEADS_DEV):
        cols, vcols = head_cols(h)
        q = q_ref[:, cols]
        top = jnp.full((1, BLOCK), NEGATIVE, f32)
        for part in range(4):
            keys = (kv_ref, pkv_ref)[part // 2][(part % 2) * HALF : (part % 2 + 1) * HALF, cols]
            sc = dot(keys, q, 1, 1) * SCORE_SCALE
            if part < 2:
                sc = jnp.where(own_mask(part * HALF), sc, NEGATIVE)
            else:
                sc = sc + prev_bias
            s_ref[FAR_KEYS + part * HALF : FAR_KEYS + (part + 1) * HALF, :] = sc
            top = jnp.maximum(top, jnp.max(sc, axis=0, keepdims=True))

        def scores(g, top):
            rows = chunk_rows(g)
            sc = chunk_bias(bias_ref, g, dot(far_ref[rows, cols], q, 1, 1) * SCORE_SCALE)
            s_ref[rows, :] = sc
            return jnp.maximum(top, jnp.max(sc, axis=0, keepdims=True))

        top = lax.fori_loop(0, CHUNKS, scores, top, unroll=2)

        def step(score, values):
            e = jnp.exp2(score - top)
            return jnp.sum(e, axis=0, keepdims=True), dot(values, e.astype(bf16), 0, 0)

        def gather(g, carry):
            a, b = step(s_ref[chunk_rows(g), :], far_ref[chunk_rows(g), vcols])
            return carry[0] + a, carry[1] + b

        start = (jnp.zeros((1, BLOCK), f32), jnp.zeros((HEAD_DIM, BLOCK), f32))
        sums, out = lax.fori_loop(0, CHUNKS, gather, start, unroll=2)
        for part in range(4):
            values = (kv_ref, pkv_ref)[part // 2][(part % 2) * HALF : (part % 2 + 1) * HALF, vcols]
            rows = slice(FAR_KEYS + part * HALF, FAR_KEYS + (part + 1) * HALF)
            a, b = step(s_ref[rows, :], values)
            sums, out = sums + a, out + b
        att_ref[:, cols] = (out / sums).T.astype(bf16)
        lse_ref[h : h + 1, :] = top + jnp.log2(sums)
    me = lax.axis_index("head")
    zl, x = me >> 2, me & 3

    def projected(dx, dz):
        columns = weight_cols(zl, x, dx, dz)[1]
        return dot(att_ref[...], w_ref[:, columns], 1, 0).astype(bf16)

    behind, ahead, late_behind, late_ahead, own = outs
    behind[:BLOCK], behind[BLOCK:] = projected(1, 1), projected(2, 0)
    ahead[:BLOCK], ahead[BLOCK:] = projected(3, 0), projected(2, 1)
    late_behind[...], late_ahead[...] = projected(1, 0), projected(3, 1)
    own[:BLOCK], own[BLOCK:] = projected(0, 0), projected(0, 1)


def step(keys, values, q, do, lse, delta, bias):
    w = jnp.exp2(bias(dot(keys, q, 1, 1) * SCORE_SCALE) - lse)
    ds = (w * (dot(values, do, 1, 1) - delta)).astype(bf16)
    dv = dot(w.astype(bf16), do, 1, 0)
    dk = dot(ds, q, 1, 0) * SCALING
    return dk, dv, dot(keys, ds, 0, 0)


def far_part(first, refs, bias_ref, near_begin, out_ref, dq_in, dq_out):
    q_ref, far_ref, lse_ref, do_ref, delta_ref = refs
    s, z, y, c = place()
    for g in range(first, first + Y):
        for dz in range(Z):
            b = block_of(z, y, c, g, dz)
            bias_ref[g * Z + dz] = jnp.where(b < near_begin, MID_BIAS, NEGATIVE)
    for h in range(HEADS_DEV):
        cols, vcols = head_cols(h)
        q, do = q_ref[:, cols], do_ref[:, cols]
        lse, delta = lse_ref[h : h + 1, :], delta_ref[h : h + 1, :]

        def body(i, acc):
            g = i + first
            rows = chunk_rows(g)
            dk, dv, dq = step(
                far_ref[rows, cols], far_ref[rows, vcols], q, do, lse, delta,
                lambda sc: chunk_bias(bias_ref, g, sc),
            )
            out_ref[chunk_rows(i), cols] = dk.astype(bf16)
            out_ref[chunk_rows(i), vcols] = dv.astype(bf16)
            return acc + dq

        acc = jnp.zeros((HEAD_DIM, BLOCK), f32) if dq_in is None else dq_in[cols, :]
        dq_out[cols, :] = lax.fori_loop(0, Y, body, acc, unroll=2)


def other_kernel(nw_hbm, q_ref, w_ref, far_ref, att_ref, lse_ref, *refs):
    grads = refs[: ZL * X]
    do_ref, delta_ref, dq_ref, weight_ref, out_ref, nw_ref, bias_ref, sems = refs[ZL * X :]
    copy = pltpu.make_async_copy(nw_hbm, nw_ref, sems.at[0])
    copy.start()
    s, z, y, c = place()
    me = lax.axis_index("head")
    zl, x = me >> 2, me & 3
    acc = jnp.zeros((BLOCK, COLS), f32)
    for i in range(ZL * X):
        device, columns = weight_cols(zl, x, i % X, i // X)
        grad = grads[i][...]
        acc = acc + dot(grad, w_ref[:, columns], 1, 1)
        term = dot(grad, att_ref[...], 0, 0).astype(bf16)
        for part in range(COLS // MIDS):
            block = device * (COLS // MIDS) + part
            bz, by = block >> 3, (block >> 1) & 3
            row = pl.multiple_of((((y - by) & 3) * Z + ((z - bz) & 3)) * MIDS, MIDS)
            piece = term[part * MIDS : (part + 1) * MIDS]

            @pl.when(c == part % 2)
            def _():
                weight_ref[pl.ds(row, MIDS), :] = piece

            @pl.when(c != part % 2)
            def _():
                out_ref[pl.ds(row, MIDS), 2 * COLS :] = piece

    do_ref[...] = acc.astype(bf16)
    for h in range(HEADS_DEV):
        cols, _ = head_cols(h)
        product = do_ref[:, cols].astype(f32) * att_ref[:, cols].astype(f32)
        delta_ref[h : h + 1, :] = jnp.sum(product.T, axis=0, keepdims=True)
    copy.wait()
    near_begin = jnp.maximum(s + 1 - nw_ref[s], 0)
    parts = (q_ref, far_ref, lse_ref, do_ref, delta_ref)
    far_part(Y, parts, bias_ref, near_begin, out_ref, None, dq_ref)


def own_kernel(
    nw_hbm, q_ref, far_ref, lse_ref, do_ref, delta_ref, dq_in, weight_ref, out_ref, dq_ref,
    nw_ref, bias_ref, sems,
):
    copy = pltpu.make_async_copy(nw_hbm, nw_ref, sems.at[0])
    copy.start()
    out_ref[:, 2 * COLS :] = weight_ref[...]
    copy.wait()
    s = place()[0]
    near_begin = jnp.maximum(s + 1 - nw_ref[s], 0)
    parts = (q_ref, far_ref, lse_ref, do_ref, delta_ref)
    far_part(0, parts, bias_ref, near_begin, out_ref, dq_in, dq_ref)


def prev_kernel(
    nw_hbm, q_ref, pkv_ref, lse_ref, do_ref, delta_ref, dq_in, rim_ref, dq_ref, nw_ref, sems
):
    copy = pltpu.make_async_copy(nw_hbm, nw_ref, sems.at[0])
    copy.start()
    copy.wait()
    s = place()[0]
    near_begin = jnp.maximum(s + 1 - nw_ref[s], 0)
    prev_bias = jnp.where(near_begin < s, 0.0, NEGATIVE)
    for h in range(HEADS_DEV):
        cols, vcols = head_cols(h)
        q, do = q_ref[:, cols], do_ref[:, cols]
        lse, delta = lse_ref[h : h + 1, :], delta_ref[h : h + 1, :]
        acc = dq_in[cols, :]
        for part in range(2):
            rows = slice(part * HALF, (part + 1) * HALF)
            dk, dv, dq = step(
                pkv_ref[rows, cols], pkv_ref[rows, vcols], q, do, lse, delta,
                lambda sc: sc + prev_bias,
            )
            rim_ref[rows, cols] = dk.astype(bf16)
            rim_ref[rows, vcols] = dv.astype(bf16)
            acc = acc + dq
        dq_ref[cols, :] = acc


def near_kernel(q_ref, kv_ref, lse_ref, do_ref, delta_ref, dq_in, dq_ref, near_ref):
    for h in range(HEADS_DEV):
        cols, vcols = head_cols(h)
        q, do = q_ref[:, cols], do_ref[:, cols]
        lse, delta = lse_ref[h : h + 1, :], delta_ref[h : h + 1, :]
        acc = dq_in[cols, :]
        for part in range(2):
            rows = slice(part * HALF, (part + 1) * HALF)
            dk, dv, dq = step(
                kv_ref[rows, cols], kv_ref[rows, vcols], q, do, lse, delta,
                lambda sc: jnp.where(own_mask(part * HALF), sc, NEGATIVE),
            )
            near_ref[rows, cols] = dk
            near_ref[rows, vcols] = dv
            acc = acc + dq
        dq_ref[:, cols] = (acc * SCALING).T.astype(bf16)


def core_kernel(own_ref, got_ref, *outs):
    def chunk(i):
        rows = slice(i * CHUNK, (i + 1) * CHUNK)
        return (wide(own_ref, rows) + wide(got_ref, rows)).astype(bf16)

    emit(chunk, outs)


def y_kernel(*refs):
    a, b = halves(*refs[:5])
    both = [h[i * MIDS : (i + 1) * MIDS].astype(bf16) for h in (a, b) for i in range(2)]
    emit(lambda i: both[i], refs[5:])


def x_kernel(own, got_behind, got_ahead, last_behind, last_ahead, keep_ref, pass_ref):
    a, b = halves(own, got_behind, got_ahead, last_behind, last_ahead)
    keep_ref[...] = a
    pass_ref[...] = b.astype(bf16)


def pair_kernel(keep_ref, got_ref, out_ref):
    out_ref[...] = (keep_ref[...] + got_ref[...].astype(f32)).astype(bf16)


def last_kernel(own, got_behind, got_ahead, last_behind, last_ahead, near_ref, rim_ref, key_ref, value_ref, weight_ref):
    total = jnp.concatenate(
        halves(own, got_behind, got_ahead, last_behind, last_ahead), axis=0
    )
    weight_ref[...] = total[:, 2 * COLS :]
    mid = total[:, : 2 * COLS] * (1.0 / POOL_MID)
    spread = jnp.broadcast_to(mid[:, None, :], (MIDS, POOL_MID, 2 * COLS)).reshape(BLOCK, 2 * COLS)
    grad = near_ref[...] + rim_ref[...].astype(f32) + spread
    key_ref[...] = grad[:, :COLS].astype(bf16)
    value_ref[...] = grad[:, COLS:].astype(bf16)


def on_device(queries, key_frames, value_frames, out_weight, out_grad, near_window, mid_start):
    dma = pltpu.SemaphoreType.DMA
    smem_window = pltpu.SMEM((Z * Y * C,), jnp.int32)
    smem_bias = pltpu.SMEM((CHUNKS * Z,), f32)
    pair_flops = 2 * HEADS_DEV * BLOCK * HEAD_DIM

    kv, mid = call(
        pool_kernel, [shape(BLOCK, 2 * COLS), shape(MIDS, 2 * COLS)], [dma((2,))], far=2
    )(key_frames, value_frames)
    ahead_g, behind_g = along_x(out_grad, 1), along_x(out_grad, -1)
    run, kv_sent = call(
        gather_kernel,
        [shape(CHUNK, 2 * COLS), shape(BLOCK, 2 * COLS)],
        after=(ahead_g, behind_g),
    )(mid, *[along_z(mid, i) for i in range(1, Z)], kv)
    ahead, behind = along_y(run, 1), along_y(run, -1)
    prev_kv = passed_along(kv_sent, 1)
    beyond_g = along_x(ahead_g, 1)
    pair = along_head(out_grad, dz=1)
    three, first, rest = call(
        part_kernel,
        [shape(3 * CHUNK, 2 * COLS), *[shape(CHUNK // 2, 2 * COLS)] * 2],
        after=(beyond_g, pair),
    )(run, ahead, behind)
    own_core = [three, along_y(first, 1), along_y(rest, -1)]
    other_core = [along_seq(v, dc=1) for v in own_core]
    ahead_p, behind_p = along_x(pair, 1), along_x(pair, -1)
    beyond_p = along_x(behind_p, -1)
    grads = [out_grad, ahead_g, beyond_g, behind_g, pair, ahead_p, beyond_p, behind_p]

    attention, lse, far, *parts = call(
        forward_kernel,
        [
            shape(BLOCK, COLS),
            shape(HEADS_DEV, BLOCK, dtype=f32),
            shape(FAR_KEYS, 2 * COLS),
            *ring_shapes(2 * BLOCK, COLS),
        ],
        [
            pltpu.VMEM((FAR_KEYS + 2 * BLOCK, BLOCK), f32),
            smem_window,
            smem_window,
            smem_bias,
            dma((2,)),
        ],
        far=2,
        flops=4 * pair_flops * 3072,
        count=2 * BLOCK * 3072,
        after=(ahead_p, behind_p),
    )(near_window, mid_start, queries, out_weight, kv, prev_kv, *own_core, *other_core)

    grad_t = shape(COLS, BLOCK, dtype=f32)
    half_rows = FAR_KEYS // 2
    attention_grad, delta, dq, weight_own, sums_other = call(
        other_kernel,
        [
            shape(BLOCK, COLS),
            shape(HEADS_DEV, BLOCK, dtype=f32),
            grad_t,
            shape(half_rows, COLS),
            shape(half_rows, SUM_COLS),
        ],
        [smem_window, smem_bias, dma((1,))],
        far=1,
        flops=10 * pair_flops * 1024 + 4 * BLOCK * 2048 * COLS,
        count=2 * BLOCK * 1024,
    )(near_window, queries, out_weight, far, attention, lse, *grads)
    sums_got = along_seq(sums_other, dc=1)
    rim, dq = call(
        prev_kernel,
        [shape(BLOCK, 2 * COLS), grad_t],
        [smem_window, dma((1,))],
        far=1,
        flops=10 * pair_flops * 512,
        count=2 * BLOCK * 512,
    )(near_window, queries, prev_kv, lse, attention_grad, delta, dq)
    rim_got = passed_along(rim, -1)
    sums_own, dq = call(
        own_kernel,
        [shape(half_rows, SUM_COLS), grad_t],
        [smem_window, smem_bias, dma((1,))],
        far=1,
        flops=10 * pair_flops * 1024,
        count=2 * BLOCK * 1024,
    )(near_window, queries, far, lse, attention_grad, delta, dq, weight_own)
    sums = call(core_kernel, ring_shapes(CHUNK, SUM_COLS))(sums_own, sums_got)
    query_grad, near_grad = call(
        near_kernel,
        [shape(BLOCK, COLS), shape(BLOCK, 2 * COLS, dtype=f32)],
        flops=10 * pair_flops * 512,
        count=2 * BLOCK * 512,
        after=(sums[0],),
    )(queries, kv, lse, attention_grad, delta, dq)

    parts = ring(parts, along_x, after=(near_grad,))
    sums = ring(sums, along_y, after=(near_grad,))
    keep, given = call(x_kernel, [shape(BLOCK, COLS, dtype=f32), shape(BLOCK, COLS)])(*parts)
    given = along_head(given, dz=1)
    sums = call(y_kernel, ring_shapes(MIDS, SUM_COLS))(*sums)
    sums = ring(sums, along_z)
    (layer_out,) = call(pair_kernel, [shape(BLOCK, COLS)])(keep, given)
    key_grad, value_grad, weight_t = call(
        last_kernel,
        [shape(BLOCK, COLS), shape(BLOCK, COLS), shape(MIDS, COLS, dtype=f32)],
    )(*sums, near_grad, rim_got)
    return layer_out, query_grad, key_grad, value_grad, weight_t.T


def solution(mesh):
    return jax.shard_map(
        on_device,
        mesh=mesh,
        in_specs=(
            P("seq", "head"),
            P("seq", "head"),
            P("seq", "head"),
            P("head", None),
            P("seq", "head"),
            P(),
            P(),
        ),
        out_specs=(
            P("seq", "head"),
            P("seq", "head"),
            P("seq", "head"),
            P("seq", "head"),
            P("head", "seq"),
        ),
        check_vma=False,
    )
```

profile of v0, /device:TPU:32, one launch (start us, length us, event | category | flops | bytes accessed | tf_op | source)
XLA Modules:
  0.0 120.0 jit_solution(4710952108567807330)
XLA Ops:
  2.2 1.7 %collective-permute-start.4 = (bf16[512,256]{1,0:T(8,128)(2,1)}, bf16[512,256]{1,0:T(8,128)(2,1)S(1)}, u32[]{:S(2)}, u32[]{:S(2)}) collective-permute-start(bf16[512,256]{1,0:T(8,128)(2,1)} %refs_6_.1), channel_id=1, source_target_pairs={{0,3},{1,0},{2,1},{3,2},{4,7},{5,4},{6,5},{7,6},{8,11},{9,8},{10,9... | collective-permute-start | bytes 786440 | tf_op jit(solution)/shard_map/ppermute | solution.py:48
  6.1 5.5 %collective-permute-start.2 = (bf16[64,512]{1,0:T(8,128)(2,1)S(1)}, bf16[64,512]{1,0:T(8,128)(2,1)S(1)}, u32[]{:S(2)}, u32[]{:S(2)}) collective-permute-start(bf16[64,512]{1,0:T(8,128)(2,1)S(1)} %get-tuple-element.53.refs_0_), channel_id=1, source_target_pairs={{0,192},{8,200},{16,208},{24,216},{32,224},{40,232},{48,240},{56,2... | collective-permute-start | bytes 196616 | tf_op jit(solution)/shard_map/ppermute | solution.py:40
  13.1 2.4 %collective-permute-start = (bf16[64,512]{1,0:T(8,128)(2,1)S(1)}, bf16[64,512]{1,0:T(8,128)(2,1)S(1)}, u32[]{:S(2)}, u32[]{:S(2)}) collective-permute-start(bf16[64,512]{1,0:T(8,128)(2,1)S(1)} %get-tuple-element.53.refs_0_), channel_id=1, source_target_pairs={{0,64},{8,72},{16,80},{24,88},{32,96},{40,104},{48,112},{56,120},{... | collective-permute-start | bytes 196616 | tf_op jit(solution)/shard_map/ppermute | solution.py:40
  17.4 3.2 %collective-permute-done.1.refs_2_ = bf16[64,512]{1,0:T(8,128)(2,1)S(1)} collective-permute-done((bf16[64,512]{1,0:T(8,128)(2,1)S(1)}, bf16[64,512]{1,0:T(8,128)(2,1)S(1)}, u32[]{:S(2)}, u32[]{:S(2)}) %collective-permute-start.1) | collective-permute-done | bytes 65568 | tf_op jit(solution)/shard_map/ppermute | solution.py:40
  20.7 2.9 %collective-permute-start.7 = (bf16[256,512]{1,0:T(8,128)(2,1)S(1)}, bf16[256,512]{1,0:T(8,128)(2,1)S(1)}, u32[]{:S(2)}, u32[]{:S(2)}) collective-permute-start(bf16[256,512]{1,0:T(8,128)(2,1)S(1)} %get-tuple-element.55.refs_0_), channel_id=1, source_target_pairs={{0,48},{8,56},{16,0},{24,8},{32,16},{40,24},{48,32},{56,40},{64,11... | collective-permute-start | bytes 786440 | tf_op jit(solution)/shard_map/ppermute | solution.py:40
  25.0 2.5 %collective-permute-done.7.refs_2_ = bf16[256,512]{1,0:T(8,128)(2,1)S(1)} collective-permute-done((bf16[256,512]{1,0:T(8,128)(2,1)S(1)}, bf16[256,512]{1,0:T(8,128)(2,1)S(1)}, u32[]{:S(2)}, u32[]{:S(2)}) %collective-permute-start.7) | collective-permute-done | bytes 262176 | tf_op jit(solution)/shard_map/ppermute | solution.py:40
  27.5 3.7 %collective-permute-done.6.refs_1_ = bf16[256,512]{1,0:T(8,128)(2,1)S(1)} collective-permute-done((bf16[256,512]{1,0:T(8,128)(2,1)S(1)}, bf16[256,512]{1,0:T(8,128)(2,1)S(1)}, u32[]{:S(2)}, u32[]{:S(2)}) %collective-permute-start.6) | collective-permute-done | bytes 262176 | tf_op jit(solution)/shard_map/ppermute | solution.py:40
  33.0 2.1 %collective-permute-start.5 = (bf16[512,512]{1,0:T(8,128)(2,1)S(1)}, bf16[512,512]{1,0:T(8,128)(2,1)S(1)}, u32[]{:S(2)}, u32[]{:S(2)}) collective-permute-start(bf16[512,512]{1,0:T(8,128)(2,1)S(1)} %get-tuple-element.54), channel_id=1, source_target_pairs={{0,8},{8,16},{16,24},{24,32},{32,40},{40,48},{48,56},{56,64},{64,7... | collective-permute-start | bytes 1572872 | tf_op jit(solution)/shard_map/ppermute | solution.py:66
  35.6 4.5 %collective-permute-done.16.refs_13_ = bf16[512,256]{1,0:T(8,128)(2,1)S(1)} collective-permute-done((bf16[512,256]{1,0:T(8,128)(2,1)S(1)}, bf16[512,256]{1,0:T(8,128)(2,1)S(1)}, u32[]{:S(2)}, u32[]{:S(2)}) %collective-permute-start.16) | collective-permute-done | bytes 262176 | tf_op jit(solution)/shard_map/ppermute | solution.py:48
  40.1 3.1 %collective-permute-done.10.refs_7_ = bf16[128,512]{1,0:T(8,128)(2,1)S(1)} collective-permute-done((bf16[128,512]{1,0:T(8,128)(2,1)S(1)}, bf16[128,512]{1,0:T(8,128)(2,1)S(1)}, u32[]{:S(2)}, u32[]{:S(2)}) %collective-permute-start.10) | collective-permute-done | bytes 131104 | tf_op jit(solution)/shard_map/ppermute | solution.py:40
  45.1 2.8 %collective-permute-start.19 = (bf16[512,256]{1,0:T(8,128)(2,1)S(1)}, bf16[512,256]{1,0:T(8,128)(2,1)S(1)}, u32[]{:S(2)}, u32[]{:S(2)}) collective-permute-start(bf16[512,256]{1,0:T(8,128)(2,1)S(1)} %collective-permute-done.16.refs_13_), channel_id=1, source_target_pairs={{0,3},{1,0},{2,1},{3,2},{4,7},{5,4},{6,5},{7,6},{8,11},{9,8},{10,9... | collective-permute-start | bytes 786440 | tf_op jit(solution)/shard_map/ppermute | solution.py:48
  47.9 8.9 %shard_map.113 = (bf16[512,256]{1,0:T(8,128)(2,1)S(1)}, f32[2,512]{1,0:T(2,128)S(1)}, bf16[2048,512]{1,0:T(8,128)(2,1)S(1)}, bf16[1024,256]{1,0:T(8,128)(2,1)S(1...) custom-call(s32[32]{0:T(128)S(1)} %copy-done.6, ...), custom_call_target="tpu_custom_call" | custom-call | flops 3221225472 | bytes 8917248 | tf_op jit(solution)/shard_map/pallas_call | solution.py:80
  56.9 6.4 %shard_map.114 = (bf16[512,256]{1,0:T(8,128)(2,1)S(1)}, f32[2,512]{1,0:T(2,128)S(1)}, f32[256,512]{1,0:T(8,128)S(1)}, bf16[1024,256]{1,0:T(8,128)(2,1)S(1)}, bf16[1024,768]{1,0:T(8,128)(2,1)S(1)}) custom-call(s32[32]{0:T(128)S(1)} %copy-done.6, bf16[512,256]{1,0:T(8,128)(2,1)S(1)} %copy-done.4, bf16[256,2048]{1,0:T(8,128)(2,1)S(1)} %copy-done.2, ...), custom_call_target="tpu_custom_call" | custom-call | flops 3758096384 | bytes 8659072 | tf_op jit(solution)/shard_map/pallas_call | solution.py:80
  65.7 2.0 %shard_map.115 = (bf16[512,512]{1,0:T(8,128)(2,1)S(1)}, f32[256,512]{1,0:T(8,128)S(1)}) custom-call(s32[32]{0:T(128)S(1)} %copy-done.6, bf16[512,256]{1,0:T(8,128)(2,1)S(1)} %copy-done.4, bf16[512,512]{1,0:T(8,128)(2,1)S(1)} %collective-permute-done.5.refs_5_.refs_2_, f32[2,512]{1,0:T(2,128)S(1)} %get-tuple-element.64.refs_5_.refs_3_.refs_2_, ...), custom_call_target="tpu_custom_call" | custom-call | flops 1342177280 | bytes 2629760 | tf_op jit(solution)/shard_map/pallas_call | solution.py:80
  67.6 3.9 %shard_map.116 = (bf16[1024,768]{1,0:T(8,128)(2,1)S(1)}, f32[256,512]{1,0:T(8,128)S(1)}) custom-call(s32[32]{0:T(128)S(1)} %copy-done.6, bf16[512,256]{1,0:T(8,128)(2,1)S(1)} %copy-done.4, bf16[2048,512]{1,0:T(8,128)(2,1)S(1)} %get-tuple-element.65.refs_3_.refs_2_, f32[2,512]{1,0:T(2,128)S(1)} %get-tuple-element.64.refs_5_.refs_3_.refs_2_, ...), custom_call_target="tpu_custom_call" | custom-call | flops 2684354560 | bytes 5775488 | tf_op jit(solution)/shard_map/pallas_call | solution.py:80
  72.0 3.2 %collective-permute-start.24 = (bf16[256,768]{1,0:T(8,128)(2,1)S(1)}, bf16[256,768]{1,0:T(8,128)(2,1)S(1)}, u32[]{:S(2)}, u32[]{:S(2)}) collective-permute-start(bf16[256,768]{1,0:T(8,128)(2,1)S(1)} %get-tuple-element.75.refs_6_), channel_id=1, source_target_pairs={{0,48},{8,56},{16,0},{24,8},{32,16},{40,24},{48,32},{56,40},{64,11... | collective-permute-start | bytes 1179656 | tf_op jit(solution)/shard_map/ppermute | solution.py:40
  75.2 2.2 %shard_map.118 = (bf16[512,256]{1,0:T(8,128)(2,1)}, f32[512,512]{1,0:T(8,128)S(1)}) custom-call(bf16[512,256]{1,0:T(8,128)(2,1)S(1)} %copy-done.4, bf16[512,512]{1,0:T(8,128)(2,1)S(1)} %get-tuple-element.52.refs_4_.refs_1_, f32[2,512]{1,0:T(2,128)S(1)} %get-tuple-element.64.refs_5_.refs_3_.refs_2_, bf16[512,256]{1,0:T(8,128)(2,1)S(1)} %get-tuple-element.67.refs_4_.refs_3_, ...), custom_call_target="tpu_custom_call" | custom-call | flops 1342177280 | bytes 2891776 | tf_op jit(solution)/shard_map/pallas_call | solution.py:80
  77.8 2.2 %collective-permute-done.18.refs_3_.refs_2_ = bf16[1024,256]{1,0:T(8,128)(2,1)S(1)} collective-permute-done((bf16[1024,256]{1,0:T(8,128)(2,1)S(1)}, bf16[1024,256]{1,0:T(8,128)(2,1)S(1)}, u32[]{:S(2)}, u32[]{:S(2)}) %collective-permute-start.18) | collective-permute-done | bytes 524320 | tf_op jit(solution)/shard_map/ppermute | solution.py:48
  84.1 3.0 %collective-permute-start.26 = (bf16[128,768]{1,0:T(8,128)(2,1)S(1)}, bf16[128,768]{1,0:T(8,128)(2,1)S(1)}, u32[]{:S(2)}, u32[]{:S(2)}) collective-permute-start(bf16[128,768]{1,0:T(8,128)(2,1)S(1)} %get-tuple-element.86), channel_id=1, source_target_pairs={{0,48},{8,56},{16,0},{24,8},{32,16},{40,24},{48,32},{56,40},{64,11... | collective-permute-start | bytes 589832 | tf_op jit(solution)/shard_map/ppermute | solution.py:40
  89.4 2.3 %collective-permute-start.23 = (bf16[512,256]{1,0:T(8,128)(2,1)S(1)}, bf16[512,256]{1,0:T(8,128)(2,1)S(1)}, u32[]{:S(2)}, u32[]{:S(2)}) collective-permute-start(bf16[512,256]{1,0:T(8,128)(2,1)S(1)} %get-tuple-element.80), channel_id=1, source_target_pairs={{0,4},{1,5},{2,6},{3,7},{4,0},{5,1},{6,2},{7,3},{8,12},{9,13},{10,... | collective-permute-start | bytes 786440 | tf_op jit(solution)/shard_map/ppermute | solution.py:48
  91.7 4.1 %collective-permute-done.26.refs_3_ = bf16[128,768]{1,0:T(8,128)(2,1)S(1)} collective-permute-done((bf16[128,768]{1,0:T(8,128)(2,1)S(1)}, bf16[128,768]{1,0:T(8,128)(2,1)S(1)}, u32[]{:S(2)}, u32[]{:S(2)}) %collective-permute-start.26) | collective-permute-done | bytes 196640 | tf_op jit(solution)/shard_map/ppermute | solution.py:40
  96.0 5.4 %collective-permute-start.28 = (bf16[64,768]{1,0:T(8,128)(2,1)S(1)}, bf16[64,768]{1,0:T(8,128)(2,1)S(1)}, u32[]{:S(2)}, u32[]{:S(2)}) collective-permute-start(bf16[64,768]{1,0:T(8,128)(2,1)S(1)} %get-tuple-element.89), channel_id=1, source_target_pairs={{0,192},{8,200},{16,208},{24,216},{32,224},{40,232},{48,240},{56,2... | collective-permute-start | bytes 294920 | tf_op jit(solution)/shard_map/ppermute | solution.py:40
  101.6 11.1 %collective-permute-done.28.refs_2_.refs_1_ = bf16[64,768]{1,0:T(8,128)(2,1)S(1)} collective-permute-done((bf16[64,768]{1,0:T(8,128)(2,1)S(1)}, bf16[64,768]{1,0:T(8,128)(2,1)S(1)}, u32[]{:S(2)}, u32[]{:S(2)}) %collective-permute-start.28) | collective-permute-done | bytes 98336 | tf_op jit(solution)/shard_map/ppermute | solution.py:40
  112.8 2.9 %collective-permute-start.31 = (bf16[32,768]{1,0:T(8,128)(2,1)S(1)}, bf16[32,768]{1,0:T(8,128)(2,1)S(1)}, u32[]{:S(2)}, u32[]{:S(2)}) collective-permute-start(bf16[32,768]{1,0:T(8,128)(2,1)S(1)} %get-tuple-element.94), channel_id=1, source_target_pairs={{0,64},{8,72},{16,80},{24,88},{32,96},{40,104},{48,112},{56,120},{... | collective-permute-start | bytes 147464 | tf_op jit(solution)/shard_map/ppermute | solution.py:40
  (72 shorter events, 27.3 us)
Async XLA Ops:
  0.6 16.5 %collective-permute-start.3 = (bf16[512,256]{1,0:T(8,128)(2,1)}, bf16[512,256]{1,0:T(8,128)(2,1)S(1)}, u32[]{:S(2)}, u32[]{:S(2)}) collective-permute-start(bf16[512,256]{1,0:T(8,128)(2,1)} %refs_6_.1), channel_id=1, source_target_pairs={{0,1},{1,2},{2,3},{3,0},{4,5},{5,6},{6,7},{7,4},{8,9},{9,10},{10,1... | collective-permute-start | bytes 786440 | tf_op jit(solution)/shard_map/ppermute | solution.py:48
  2.2 18.4 %collective-permute-start.4 = (bf16[512,256]{1,0:T(8,128)(2,1)}, bf16[512,256]{1,0:T(8,128)(2,1)S(1)}, u32[]{:S(2)}, u32[]{:S(2)}) collective-permute-start(bf16[512,256]{1,0:T(8,128)(2,1)} %refs_6_.1), channel_id=1, source_target_pairs={{0,3},{1,0},{2,1},{3,2},{4,7},{5,4},{6,5},{7,6},{8,11},{9,8},{10,9... | collective-permute-start | bytes 786440 | tf_op jit(solution)/shard_map/ppermute | solution.py:48
  6.1 9.3 %collective-permute-start.2 = (bf16[64,512]{1,0:T(8,128)(2,1)S(1)}, bf16[64,512]{1,0:T(8,128)(2,1)S(1)}, u32[]{:S(2)}, u32[]{:S(2)}) collective-permute-start(bf16[64,512]{1,0:T(8,128)(2,1)S(1)} %get-tuple-element.53.refs_0_), channel_id=1, source_target_pairs={{0,192},{8,200},{16,208},{24,216},{32,224},{40,232},{48,240},{56,2... | collective-permute-start | bytes 196616 | tf_op jit(solution)/shard_map/ppermute | solution.py:40
  11.6 9.0 %collective-permute-start.1 = (bf16[64,512]{1,0:T(8,128)(2,1)S(1)}, bf16[64,512]{1,0:T(8,128)(2,1)S(1)}, u32[]{:S(2)}, u32[]{:S(2)}) collective-permute-start(bf16[64,512]{1,0:T(8,128)(2,1)S(1)} %get-tuple-element.53.refs_0_), channel_id=1, source_target_pairs={{0,128},{8,136},{16,144},{24,152},{32,160},{40,168},{48,176},{56,1... | collective-permute-start | bytes 196616 | tf_op jit(solution)/shard_map/ppermute | solution.py:40
  15.4 9.5 %collective-permute-start.9 = (bf16[512,256]{1,0:T(8,128)(2,1)}, bf16[512,256]{1,0:T(8,128)(2,1)S(1)}, u32[]{:S(2)}, u32[]{:S(2)}) collective-permute-start(bf16[512,256]{1,0:T(8,128)(2,1)} %refs_6_.1), channel_id=1, source_target_pairs={{0,4},{1,5},{2,6},{3,7},{4,0},{5,1},{6,2},{7,3},{8,12},{9,13},{10,... | collective-permute-start | bytes 786440 | tf_op jit(solution)/shard_map/ppermute | solution.py:48
  17.1 7.9 %collective-permute-start.8 = (bf16[512,256]{1,0:T(8,128)(2,1)S(1)}, bf16[512,256]{1,0:T(8,128)(2,1)S(1)}, u32[]{:S(2)}, u32[]{:S(2)}) collective-permute-start(bf16[512,256]{1,0:T(8,128)(2,1)S(1)} %collective-permute-done.3.refs_5_.refs_7_), channel_id=1, source_target_pairs={{0,1},{1,2},{2,3},{3,0},{4,5},{5,6},{6,7},{7,4},{8,9},{9,10},{10,1... | collective-permute-start | bytes 786440 | tf_op jit(solution)/shard_map/ppermute | solution.py:48
  23.6 7.6 %collective-permute-start.6 = (bf16[256,512]{1,0:T(8,128)(2,1)S(1)}, bf16[256,512]{1,0:T(8,128)(2,1)S(1)}, u32[]{:S(2)}, u32[]{:S(2)}) collective-permute-start(bf16[256,512]{1,0:T(8,128)(2,1)S(1)} %get-tuple-element.55.refs_0_), channel_id=1, source_target_pairs={{0,16},{8,24},{16,32},{24,40},{32,48},{40,56},{48,0},{56,8},{64,80... | collective-permute-start | bytes 786440 | tf_op jit(solution)/shard_map/ppermute | solution.py:40
  31.2 16.7 %collective-permute-start.12 = (bf16[768,512]{1,0:T(8,128)(2,1)S(1)}, bf16[768,512]{1,0:T(8,128)(2,1)S(1)}, u32[]{:S(2)}, u32[]{:S(2)}) collective-permute-start(bf16[768,512]{1,0:T(8,128)(2,1)S(1)} %get-tuple-element.56.refs_6_), channel_id=1, source_target_pairs={{0,8},{8,0},{16,24},{24,16},{32,40},{40,32},{48,56},{56,48},{64,72... | collective-permute-start | bytes 2359304 | tf_op jit(solution)/shard_map/ppermute | solution.py:40
  31.3 8.7 %collective-permute-start.16 = (bf16[512,256]{1,0:T(8,128)(2,1)S(1)}, bf16[512,256]{1,0:T(8,128)(2,1)S(1)}, u32[]{:S(2)}, u32[]{:S(2)}) collective-permute-start(bf16[512,256]{1,0:T(8,128)(2,1)S(1)} %collective-permute-done.9.refs_4_.refs_10_), channel_id=1, source_target_pairs={{0,3},{1,0},{2,1},{3,2},{4,7},{5,4},{6,5},{7,6},{8,11},{9,8},{10,9... | collective-permute-start | bytes 786440 | tf_op jit(solution)/shard_map/ppermute | solution.py:48
  33.0 14.9 %collective-permute-start.5 = (bf16[512,512]{1,0:T(8,128)(2,1)S(1)}, bf16[512,512]{1,0:T(8,128)(2,1)S(1)}, u32[]{:S(2)}, u32[]{:S(2)}) collective-permute-start(bf16[512,512]{1,0:T(8,128)(2,1)S(1)} %get-tuple-element.54), channel_id=1, source_target_pairs={{0,8},{8,16},{16,24},{24,32},{32,40},{40,48},{48,56},{56,64},{64,7... | collective-permute-start | bytes 1572872 | tf_op jit(solution)/shard_map/ppermute | solution.py:66
  35.0 10.1 %collective-permute-start.15 = (bf16[512,256]{1,0:T(8,128)(2,1)S(1)}, bf16[512,256]{1,0:T(8,128)(2,1)S(1)}, u32[]{:S(2)}, u32[]{:S(2)}) collective-permute-start(bf16[512,256]{1,0:T(8,128)(2,1)S(1)} %collective-permute-done.9.refs_4_.refs_10_), channel_id=1, source_target_pairs={{0,1},{1,2},{2,3},{3,0},{4,5},{5,6},{6,7},{7,4},{8,9},{9,10},{10,1... | collective-permute-start | bytes 786440 | tf_op jit(solution)/shard_map/ppermute | solution.py:48
  45.1 11.8 %collective-permute-start.19 = (bf16[512,256]{1,0:T(8,128)(2,1)S(1)}, bf16[512,256]{1,0:T(8,128)(2,1)S(1)}, u32[]{:S(2)}, u32[]{:S(2)}) collective-permute-start(bf16[512,256]{1,0:T(8,128)(2,1)S(1)} %collective-permute-done.16.refs_13_), channel_id=1, source_target_pairs={{0,3},{1,0},{2,1},{3,2},{4,7},{5,4},{6,5},{7,6},{8,11},{9,8},{10,9... | collective-permute-start | bytes 786440 | tf_op jit(solution)/shard_map/ppermute | solution.py:48
  63.3 8.2 %collective-permute-start.20 = (bf16[1024,768]{1,0:T(8,128)(2,1)S(1)}, bf16[1024,768]{1,0:T(8,128)(2,1)S(1)}, u32[]{:S(2)}, u32[]{:S(2)}) collective-permute-start(bf16[1024,768]{1,0:T(8,128)(2,1)S(1)} %get-tuple-element.74), channel_id=1, source_target_pairs={{0,8},{8,0},{16,24},{24,16},{32,40},{40,32},{48,56},{56,48},{64,72... | collective-permute-start | bytes 4718600 | tf_op jit(solution)/shard_map/ppermute | solution.py:40
  63.6 14.1 %collective-permute-start.17 = (bf16[1024,256]{1,0:T(8,128)(2,1)S(1)}, bf16[1024,256]{1,0:T(8,128)(2,1)S(1)}, u32[]{:S(2)}, u32[]{:S(2)}) collective-permute-start(bf16[1024,256]{1,0:T(8,128)(2,1)S(1)} %get-tuple-element.60), channel_id=1, source_target_pairs={{0,3},{1,0},{2,1},{3,2},{4,7},{5,4},{6,5},{7,6},{8,11},{9,8},{10,9... | collective-permute-start | bytes 1572872 | tf_op jit(solution)/shard_map/ppermute | solution.py:48
  64.9 15.1 %collective-permute-start.18 = (bf16[1024,256]{1,0:T(8,128)(2,1)S(1)}, bf16[1024,256]{1,0:T(8,128)(2,1)S(1)}, u32[]{:S(2)}, u32[]{:S(2)}) collective-permute-start(bf16[1024,256]{1,0:T(8,128)(2,1)S(1)} %get-tuple-element.61), channel_id=1, source_target_pairs={{0,1},{1,2},{2,3},{3,0},{4,5},{5,6},{6,7},{7,4},{8,9},{9,10},{10,1... | collective-permute-start | bytes 1572872 | tf_op jit(solution)/shard_map/ppermute | solution.py:48
  71.9 12.1 %collective-permute-start.25 = (bf16[256,768]{1,0:T(8,128)(2,1)S(1)}, bf16[256,768]{1,0:T(8,128)(2,1)S(1)}, u32[]{:S(2)}, u32[]{:S(2)}) collective-permute-start(bf16[256,768]{1,0:T(8,128)(2,1)S(1)} %get-tuple-element.83), channel_id=1, source_target_pairs={{0,16},{8,24},{16,32},{24,40},{32,48},{40,56},{48,0},{56,8},{64,80... | collective-permute-start | bytes 1179656 | tf_op jit(solution)/shard_map/ppermute | solution.py:40
  72.0 12.0 %collective-permute-start.24 = (bf16[256,768]{1,0:T(8,128)(2,1)S(1)}, bf16[256,768]{1,0:T(8,128)(2,1)S(1)}, u32[]{:S(2)}, u32[]{:S(2)}) collective-permute-start(bf16[256,768]{1,0:T(8,128)(2,1)S(1)} %get-tuple-element.75.refs_6_), channel_id=1, source_target_pairs={{0,48},{8,56},{16,0},{24,8},{32,16},{40,24},{48,32},{56,40},{64,11... | collective-permute-start | bytes 1179656 | tf_op jit(solution)/shard_map/ppermute | solution.py:40
  80.5 8.7 %collective-permute-start.22 = (bf16[512,256]{1,0:T(8,128)(2,1)S(1)}, bf16[512,256]{1,0:T(8,128)(2,1)S(1)}, u32[]{:S(2)}, u32[]{:S(2)}) collective-permute-start(bf16[512,256]{1,0:T(8,128)(2,1)S(1)} %get-tuple-element.78), channel_id=1, source_target_pairs={{0,1},{1,2},{2,3},{3,0},{4,5},{5,6},{6,7},{7,4},{8,9},{9,10},{10,1... | collective-permute-start | bytes 786440 | tf_op jit(solution)/shard_map/ppermute | solution.py:48
  82.2 34.2 %collective-permute-start.32 = (bf16[512,512]{1,0:T(8,128)(2,1)S(1)}, bf16[512,512]{1,0:T(8,128)(2,1)S(1)}, u32[]{:S(2)}, u32[]{:S(2)}) collective-permute-start(bf16[512,512]{1,0:T(8,128)(2,1)S(1)} %get-tuple-element.95), channel_id=1, source_target_pairs={{8,0},{16,8},{24,16},{32,24},{40,32},{48,40},{56,48},{64,56},{72,6... | collective-permute-start | bytes 1572872 | tf_op jit(solution)/shard_map/ppermute | solution.py:66
  84.1 11.7 %collective-permute-start.26 = (bf16[128,768]{1,0:T(8,128)(2,1)S(1)}, bf16[128,768]{1,0:T(8,128)(2,1)S(1)}, u32[]{:S(2)}, u32[]{:S(2)}) collective-permute-start(bf16[128,768]{1,0:T(8,128)(2,1)S(1)} %get-tuple-element.86), channel_id=1, source_target_pairs={{0,48},{8,56},{16,0},{24,8},{32,16},{40,24},{48,32},{56,40},{64,11... | collective-permute-start | bytes 589832 | tf_op jit(solution)/shard_map/ppermute | solution.py:40
  87.1 8.7 %collective-permute-start.27 = (bf16[128,768]{1,0:T(8,128)(2,1)S(1)}, bf16[128,768]{1,0:T(8,128)(2,1)S(1)}, u32[]{:S(2)}, u32[]{:S(2)}) collective-permute-start(bf16[128,768]{1,0:T(8,128)(2,1)S(1)} %get-tuple-element.87), channel_id=1, source_target_pairs={{0,16},{8,24},{16,32},{24,40},{32,48},{40,56},{48,0},{56,8},{64,80... | collective-permute-start | bytes 589832 | tf_op jit(solution)/shard_map/ppermute | solution.py:40
  89.4 26.3 %collective-permute-start.23 = (bf16[512,256]{1,0:T(8,128)(2,1)S(1)}, bf16[512,256]{1,0:T(8,128)(2,1)S(1)}, u32[]{:S(2)}, u32[]{:S(2)}) collective-permute-start(bf16[512,256]{1,0:T(8,128)(2,1)S(1)} %get-tuple-element.80), channel_id=1, source_target_pairs={{0,4},{1,5},{2,6},{3,7},{4,0},{5,1},{6,2},{7,3},{8,12},{9,13},{10,... | collective-permute-start | bytes 786440 | tf_op jit(solution)/shard_map/ppermute | solution.py:48
  96.0 16.7 %collective-permute-start.28 = (bf16[64,768]{1,0:T(8,128)(2,1)S(1)}, bf16[64,768]{1,0:T(8,128)(2,1)S(1)}, u32[]{:S(2)}, u32[]{:S(2)}) collective-permute-start(bf16[64,768]{1,0:T(8,128)(2,1)S(1)} %get-tuple-element.89), channel_id=1, source_target_pairs={{0,192},{8,200},{16,208},{24,216},{32,224},{40,232},{48,240},{56,2... | collective-permute-start | bytes 294920 | tf_op jit(solution)/shard_map/ppermute | solution.py:40
  101.4 11.3 %collective-permute-start.29 = (bf16[64,768]{1,0:T(8,128)(2,1)S(1)}, bf16[64,768]{1,0:T(8,128)(2,1)S(1)}, u32[]{:S(2)}, u32[]{:S(2)}) collective-permute-start(bf16[64,768]{1,0:T(8,128)(2,1)S(1)} %get-tuple-element.90), channel_id=1, source_target_pairs={{0,64},{8,72},{16,80},{24,88},{32,96},{40,104},{48,112},{56,120},{... | collective-permute-start | bytes 294920 | tf_op jit(solution)/shard_map/ppermute | solution.py:40
  (16 other events, 240.3 us)
where the time goes:
time: 121 us; the launch traced here: 120 us
  starting transfers between devices  48.4 us (40%)
  waiting for transfers between devices  42.4 us (35%)
  Pallas kernels  26.5 us (22%)
  local copies, waits for them, and re-layouts  1.92 us (2%)
    ppermute x19, waiting for transfers between devices, along_seq(): return lax.ppermute(value, 'seq', pairs)  31.8 us
    ppermute x19, starting transfers between devices, along_seq(): return lax.ppermute(value, 'seq', pairs)  28.4 us
    pallas_call x16, Pallas kernels, run(): pl.pallas_call(body, out_shape=list(outs), in_specs=[pl.BlockSpec(memory_...  26.5 us
    ppermute x12, starting transfers between devices, along_head(): return lax.ppermute(value, 'head', pairs)  16.6 us
    ppermute x12, waiting for transfers between devices, along_head(): return lax.ppermute(value, 'head', pairs)  10.5 us
    ppermute x2, starting transfers between devices, passed_along(): lax.ppermute(value, 'seq', [(source, source + steps) for source in range(...  3.36 us
  transfers between devices with their start and end apart: 33, of which 16 were waited for; matrix products, arithmetic and copies ran while one was open for 0% of the time, Pallas kernels for 16%

commit v1 on v0

v1 whole, which is shorter than its diff:
```python
import functools
import math

import jax
import jax.numpy as jnp
from jax import lax
from jax.experimental import pallas as pl
from jax.experimental.pallas import tpu as pltpu
from jax.sharding import PartitionSpec as P

HEAD_DIM = 128
BLOCK = 512
POOL_MID = 8
MIDS = BLOCK // POOL_MID
HEADS_DEV = 2
COLS = HEADS_DEV * HEAD_DIM
Z, Y, C = 4, 4, 2
ZL, X = 2, 4
CHUNK = Z * MIDS
CHUNKS = Y * C
FAR_KEYS = CHUNKS * CHUNK
HALF = BLOCK // 2
SUM_COLS = 3 * COLS

NEGATIVE = -1e30
SCALING = HEAD_DIM ** (-0.5)
SCORE_SCALE = SCALING * math.log2(math.e)
MID_BIAS = math.log2(POOL_MID)

bf16 = jnp.bfloat16
f32 = jnp.float32


def along_seq(value, dz=0, dy=0, dc=0):
    pairs = []
    for z in range(Z):
        for y in range(Y):
            for c in range(C):
                target = (((z + dz) % Z) * Y + (y + dy) % Y) * C + (c + dc) % C
                pairs.append(((z * Y + y) * C + c, target))
    return lax.ppermute(value, "seq", pairs)


def along_head(value, dz=0, dx=0):
    pairs = []
    for z in range(ZL):
        for x in range(X):
            pairs.append((z * X + x, ((z + dz) % ZL) * X + (x + dx) % X))
    return lax.ppermute(value, "head", pairs)


def along_z(value, step):
    return along_seq(value, dz=step)


def along_y(value, step):
    return along_seq(value, dy=step)


def along_x(value, step):
    return along_head(value, dx=step)


def passed_along(value, steps):
    count = Z * Y * C
    initial, last = (max(0, -steps), min(count, count - steps))
    return lax.ppermute(value, "seq", [(source, source + steps) for source in range(initial, last)])


def shape(*dims, dtype=bf16):
    return jax.ShapeDtypeStruct(dims, dtype)


def call(kernel, outs, scratch=(), far=0, flops=0, count=0, after=()):
    def run(*args):
        moved = sum(a.size * a.dtype.itemsize for a in (*args, *outs))

        def body(*refs):
            kernel(*refs[: len(args)], *refs[len(args) + len(after) :])

        return pl.pallas_call(
            body,
            out_shape=list(outs),
            in_specs=[pl.BlockSpec(memory_space=pltpu.HBM)] * far
            + [pl.BlockSpec(memory_space=pltpu.VMEM)] * (len(args) - far)
            + [pl.BlockSpec(memory_space=pl.ANY)] * len(after),
            out_specs=[pl.BlockSpec(memory_space=pltpu.VMEM)] * len(outs),
            scratch_shapes=list(scratch),
            cost_estimate=pl.CostEstimate(flops=flops, bytes_accessed=moved, transcendentals=count),
            compiler_params=pltpu.CompilerParams(vmem_limit_bytes=26 * 1024 * 1024),
        )(*args, *after)

    return run


def place():
    s = lax.axis_index("seq")
    return s, s >> 3, (s >> 1) & 3, s & 1


def block_of(z, y, c, group, dz):
    core = (c + (group >> 2)) & 1
    return ((z - dz) & 3) * 8 + ((y - group) & 3) * 2 + core


def behind_y(i):
    return i ^ (i >> 1)


def dot(a, b, da, db):
    return lax.dot_general(a, b, (((da,), (db,)), ((), ())), preferred_element_type=f32)


def wide(ref, rows):
    return ref[rows].astype(f32)


def emit(chunk, outs):
    behind, ahead, late_behind, late_ahead, own = outs
    h = chunk(0).shape[0] // 2
    behind[:h], behind[h:] = chunk(1)[h:], chunk(2)[:h]
    ahead[:h], ahead[h:] = chunk(3)[:h], chunk(2)[h:]
    late_behind[...], late_ahead[...] = chunk(1)[:h], chunk(3)[h:]
    own[...] = chunk(0)


def ring_shapes(rows, width):
    h = rows // 2
    return [shape(rows, width)] * 2 + [shape(h, width)] * 2 + [shape(rows, width)]


def turn_kernel(late_behind, late_ahead, got_behind, got_ahead, out_behind, out_ahead):
    h = late_behind.shape[0]
    rest, all_rows = slice(h, 2 * h), slice(0, h)
    out_behind[...] = (wide(late_behind, all_rows) + wide(got_behind, rest)).astype(bf16)
    out_ahead[...] = (wide(late_ahead, all_rows) + wide(got_ahead, rest)).astype(bf16)


def ring(parts, along, after=()):
    behind, ahead, late_behind, late_ahead, own = parts
    got_behind, got_ahead = along(behind, -1), along(ahead, 1)
    turned = [shape(*late_behind.shape)] * 2
    out_behind, out_ahead = call(turn_kernel, turned, after=after)(
        late_behind, late_ahead, got_behind, got_ahead
    )
    sent = along(out_behind, -1), along(out_ahead, 1)
    return (own, got_behind, got_ahead, *sent), out_behind


def halves(own, got_behind, got_ahead, last_behind, last_ahead):
    h = last_behind.shape[0]
    first, rest = slice(0, h), slice(h, 2 * h)
    a = wide(own, first) + wide(got_ahead, first) + wide(last_behind, first)
    b = wide(own, rest) + wide(got_behind, first) + wide(last_ahead, first)
    return a, b


def pool_kernel(kv_ref, mid_ref):
    row = lax.broadcasted_iota(jnp.int32, (MIDS, BLOCK), 0)
    col = lax.broadcasted_iota(jnp.int32, (MIDS, BLOCK), 1)
    mean = jnp.where(row == col // POOL_MID, 1.0 / POOL_MID, 0.0).astype(bf16)
    mid_ref[...] = dot(mean, kv_ref[...], 1, 0).astype(bf16)


def gather_kernel(mid_ref, a, b, c, grad_ref, pair_ref, run_ref, grads_out):
    for i, ref in enumerate((mid_ref, a, b, c)):
        run_ref[i * MIDS : (i + 1) * MIDS] = ref[...]
    grads_out[:BLOCK] = grad_ref[...]
    grads_out[BLOCK:] = pair_ref[...]


def part_kernel(run_ref, ahead_ref, behind_ref, kv_ref, first_ref, rest_ref, three_ref, keys_out):
    h = CHUNK // 2
    first_ref[...] = ahead_ref[:h]
    rest_ref[...] = behind_ref[h:]
    for i, ref in enumerate((run_ref, ahead_ref, behind_ref)):
        three_ref[i * CHUNK : (i + 1) * CHUNK] = ref[...]
    keys_out[...] = kv_ref[:, :COLS]


def join_kernel(first, rest, grads_1, grads_3, last_ref, own_out, pair_out):
    last_ref[: CHUNK // 2] = first[...]
    last_ref[CHUNK // 2 :] = rest[...]
    own_out[...] = grads_1[:BLOCK]
    pair_out[...] = grads_3[BLOCK:]


def own_mask(first_key):
    key = lax.broadcasted_iota(jnp.int32, (HALF, BLOCK), 0) + first_key
    query = lax.broadcasted_iota(jnp.int32, (HALF, BLOCK), 1)
    return key <= query


def chunk_exponents(bias_ref, g, product, top):
    return jnp.concatenate(
        [
            product[d * MIDS : (d + 1) * MIDS] * SCORE_SCALE + (bias_ref[g * Z + d] - top)
            for d in range(Z)
        ],
        axis=0,
    )


def chunk_rows(g):
    return pl.ds(pl.multiple_of(g * CHUNK, CHUNK), CHUNK)


def head_cols(h):
    return slice(h * HEAD_DIM, (h + 1) * HEAD_DIM), slice(
        COLS + h * HEAD_DIM, COLS + (h + 1) * HEAD_DIM
    )


def weight_cols(zl, x, dx, dz):
    device = ((zl + dz) & 1) * X + ((x - dx) & 3)
    return device, pl.ds(pl.multiple_of(device * COLS, COLS), COLS)


def effective(near_begin, mid_begin, chunks, bias_ref):
    s, z, y, c = place()
    row = lax.broadcasted_iota(jnp.int32, (CHUNK, CHUNK), 0)
    col = lax.broadcasted_iota(jnp.int32, (CHUNK, CHUNK), 1)
    same = jnp.where(row == col, 1.0, 0.0)
    mean = jnp.where(row // POOL_MID == col // POOL_MID, 1.0 / POOL_MID, 0.0)
    for i, (core, number, mids_ref, mids_row, far_ref, far_row) in enumerate(chunks):
        picks = []
        for dz in range(Z):
            b = block_of(z, y, c, core * Y + behind_y(number), dz)
            bias_ref[i * Z + dz] = jnp.where(b < near_begin, MID_BIAS, NEGATIVE)
            far = jnp.where(b < mid_begin, 1.0, 0.0)
            rows = slice(dz * MIDS, (dz + 1) * MIDS)
            picks.append(same[rows] + far * (mean[rows] - same[rows]))
        pick = jnp.concatenate(picks, axis=0).astype(bf16)
        mids = mids_ref[mids_row : mids_row + CHUNK, :]
        far_ref[far_row : far_row + CHUNK, :] = dot(pick, mids, 1, 0).astype(bf16)


def window(nw_hbm, ms_hbm, nw_ref, ms_ref, sems):
    copies = [
        pltpu.make_async_copy(a, b, sems.at[i])
        for i, (a, b) in enumerate(((nw_hbm, nw_ref), (ms_hbm, ms_ref)))
    ]
    for copy in copies:
        copy.start()
    for copy in copies:
        copy.wait()
    s = place()[0]
    near_begin = jnp.maximum(s + 1 - nw_ref[s], 0)
    return near_begin, jnp.minimum(ms_ref[s], near_begin)


def level(h, q_t, near_ref, near_mask, near_bias, chunks, bias_ref, s_ref):
    cols, vcols = head_cols(h)
    top = jnp.full((1, BLOCK), 0.1 * NEGATIVE, f32)

    def highest(top, product, bias):
        return jnp.maximum(top, jnp.max(product, axis=0, keepdims=True) * SCORE_SCALE + bias)

    for part in range(2):
        rows = slice(part * HALF, (part + 1) * HALF)
        product = dot(near_ref[rows, cols], q_t, 1, 0)
        if near_mask:
            product = jnp.where(own_mask(part * HALF), product, NEGATIVE)
        s_ref[rows, :] = product
        top = highest(top, product, near_bias)

    for g, (_, _, _, _, far_ref, row) in enumerate(chunks):
        product = dot(far_ref[row : row + CHUNK, cols], q_t, 1, 0)
        s_ref[BLOCK + g * CHUNK : BLOCK + (g + 1) * CHUNK, :] = product
        for d in range(Z):
            top = highest(top, product[d * MIDS : (d + 1) * MIDS], bias_ref[g * Z + d])

    def values_of(exponents, values):
        e = jnp.exp2(exponents)
        return jnp.sum(e, axis=0, keepdims=True), dot(values, e.astype(bf16), 0, 0)

    sums, out = jnp.zeros((1, BLOCK), f32), jnp.zeros((HEAD_DIM, BLOCK), f32)
    for g, (_, _, _, _, far_ref, row) in enumerate(chunks):
        product = s_ref[BLOCK + g * CHUNK : BLOCK + (g + 1) * CHUNK, :]
        exponents = chunk_exponents(bias_ref, g, product, top)
        a, b = values_of(exponents, far_ref[row : row + CHUNK, vcols])
        sums, out = sums + a, out + b
    for part in range(2):
        rows = slice(part * HALF, (part + 1) * HALF)
        a, b = values_of(s_ref[rows, :] * SCORE_SCALE + (near_bias - top), near_ref[rows, vcols])
        sums, out = sums + a, out + b
    return top, sums, out


def first_kernel(
    nw_hbm, ms_hbm, q_ref, kv_ref, mids_ref, far_ref, top_ref, sums_ref, out_ref,
    s_ref, nw_ref, ms_ref, bias_ref, sems,
):
    near_begin, mid_begin = window(nw_hbm, ms_hbm, nw_ref, ms_ref, sems)
    chunks = [(0, i, mids_ref, i * CHUNK, far_ref, i * CHUNK) for i in range(3)]
    effective(near_begin, mid_begin, chunks, bias_ref)
    for h in range(HEADS_DEV):
        top, sums, out = level(
            h, q_ref[:, head_cols(h)[0]].T, kv_ref, True, 0.0, chunks, bias_ref, s_ref
        )
        top_ref[h : h + 1, :] = top
        sums_ref[h : h + 1, :] = sums
        out_ref[head_cols(h)[0], :] = out


def second_kernel(
    nw_hbm, ms_hbm, q_ref, w_ref, pk_ref, pv_ref, last_ref, three_ref, other_ref, far_own_ref,
    top_ref, sums_ref, out_ref, far_last_ref, far_ref, pkv_ref, att_ref, lse_ref, behind, ahead, late_behind, late_ahead, own,
    s_ref, nw_ref, ms_ref, bias_ref, sems,
):
    near_begin, mid_begin = window(nw_hbm, ms_hbm, nw_ref, ms_ref, sems)
    chunks = [(0, 3, last_ref, 0, far_last_ref, 3 * CHUNK)]
    chunks += [(1, i, three_ref, i * CHUNK, far_ref, i * CHUNK) for i in range(3)]
    chunks += [(1, 3, other_ref, 0, far_ref, 3 * CHUNK)]
    effective(near_begin, mid_begin, chunks, bias_ref)
    far_last_ref[: 3 * CHUNK] = far_own_ref[...]
    pkv_ref[:, :COLS], pkv_ref[:, COLS:] = pk_ref[...], pv_ref[...]
    prev_bias = jnp.where(near_begin < place()[0], 0.0, NEGATIVE)
    for h in range(HEADS_DEV):
        cols = head_cols(h)[0]
        top, sums, out = level(
            h, q_ref[:, cols].T, pkv_ref, False, prev_bias, chunks, bias_ref, s_ref
        )
        top_a = top_ref[h : h + 1, :]
        both = jnp.maximum(top, top_a)
        scale, scale_a = jnp.exp2(top - both), jnp.exp2(top_a - both)
        sums = sums * scale + sums_ref[h : h + 1, :] * scale_a
        out = out * scale + out_ref[cols, :] * scale_a
        att_ref[:, cols] = (out / sums).T.astype(bf16)
        lse_ref[h : h + 1, :] = both + jnp.log2(sums)
    me = lax.axis_index("head")
    zl, x = me >> 2, me & 3

    def projected(dx, dz):
        columns = weight_cols(zl, x, dx, dz)[1]
        return dot(att_ref[...], w_ref[:, columns], 1, 0).astype(bf16)

    behind[:BLOCK], behind[BLOCK:] = projected(1, 1), projected(2, 0)
    ahead[:BLOCK], ahead[BLOCK:] = projected(3, 0), projected(2, 1)
    late_behind[...], late_ahead[...] = projected(1, 0), projected(3, 1)
    own[:BLOCK], own[BLOCK:] = projected(0, 0), projected(0, 1)


def step(keys, values, q, do, q_t, do_t, delta, exponents):
    w = jnp.exp2(exponents(dot(keys, q_t, 1, 0)))
    ds = (w * (dot(values, do_t, 1, 0) - delta)).astype(bf16)
    dv = dot(w.astype(bf16), do, 1, 0)
    dk = dot(ds, q, 1, 0) * SCALING
    return dk, dv, dot(keys, ds, 0, 0)


def far_part(first, refs, bias_ref, near_begin, out_ref, dq_in, dq_out):
    q_ref, far_ref, lse_ref, do_ref, delta_ref = refs
    s, z, y, c = place()
    for i in range(Y):
        for dz in range(Z):
            b = block_of(z, y, c, first + behind_y(i), dz)
            bias_ref[i * Z + dz] = jnp.where(b < near_begin, MID_BIAS, NEGATIVE)
    for h in range(HEADS_DEV):
        cols, vcols = head_cols(h)
        q, do = q_ref[:, cols], do_ref[:, cols]
        q_t, do_t = q.T, do.T
        lse, delta = lse_ref[h : h + 1, :], delta_ref[h : h + 1, :]

        def body(i, acc):
            rows = chunk_rows(i)
            dk, dv, dq = step(
                far_ref[rows, cols], far_ref[rows, vcols], q, do, q_t, do_t, delta,
                lambda p: chunk_exponents(bias_ref, i, p, lse),
            )
            target = chunk_rows(behind_y(i))
            out_ref[target, cols] = dk.astype(bf16)
            out_ref[target, vcols] = dv.astype(bf16)
            return acc + dq

        dq_out[cols, :] = lax.fori_loop(0, Y, body, dq_in[cols, :], unroll=2)


def project_kernel(w_ref, att_ref, *refs):
    grads = refs[: X + 1]
    do_ref, delta_ref, own_ref, other_ref = refs[X + 1 :]
    s, z, y, c = place()
    me = lax.axis_index("head")
    zl, x = me >> 2, me & 3
    acc = jnp.zeros((BLOCK, COLS), f32)
    for i in range(ZL * X):
        device, columns = weight_cols(zl, x, i % X, i // X)
        dx, dz = i % X, i // X
        if dx == 2:
            grad = grads[2 + dz][...]
        else:
            grad = grads[dx + dx // 3][dz * BLOCK : (dz + 1) * BLOCK]
        acc = acc + dot(grad, w_ref[:, columns], 1, 1)
        term = dot(grad, att_ref[...], 0, 0).astype(bf16)
        for part in range(COLS // MIDS):
            block = device * (COLS // MIDS) + part
            bz, by = block >> 3, (block >> 1) & 3
            row = pl.multiple_of((((y - by) & 3) * Z + ((z - bz) & 3)) * MIDS, MIDS)
            piece = term[part * MIDS : (part + 1) * MIDS]

            @pl.when(c == part % 2)
            def _():
                own_ref[pl.ds(row, MIDS), :] = piece

            @pl.when(c != part % 2)
            def _():
                other_ref[pl.ds(row, MIDS), :] = piece

    do_ref[...] = acc.astype(bf16)
    for h in range(HEADS_DEV):
        cols, _ = head_cols(h)
        product = do_ref[:, cols].astype(f32) * att_ref[:, cols].astype(f32)
        delta_ref[h : h + 1, :] = jnp.sum(product.T, axis=0, keepdims=True)


def far_kernel(
    first, nw_hbm, q_ref, far_ref, lse_ref, do_ref, delta_ref, dq_in, weight_ref, out_ref, dq_ref,
    nw_ref, bias_ref, sems,
):
    copy = pltpu.make_async_copy(nw_hbm, nw_ref, sems.at[0])
    copy.start()
    out_ref[:, 2 * COLS :] = weight_ref[...]
    copy.wait()
    s = place()[0]
    near_begin = jnp.maximum(s + 1 - nw_ref[s], 0)
    parts = (q_ref, far_ref, lse_ref, do_ref, delta_ref)
    far_part(first, parts, bias_ref, near_begin, out_ref, dq_in, dq_ref)


def prev_kernel(
    nw_hbm, q_ref, pkv_ref, lse_ref, do_ref, delta_ref, rim_ref, dq_ref, nw_ref, sems
):
    copy = pltpu.make_async_copy(nw_hbm, nw_ref, sems.at[0])
    copy.start()
    copy.wait()
    s = place()[0]
    near_begin = jnp.maximum(s + 1 - nw_ref[s], 0)
    prev_bias = jnp.where(near_begin < s, 0.0, NEGATIVE)
    for h in range(HEADS_DEV):
        cols, vcols = head_cols(h)
        q, do = q_ref[:, cols], do_ref[:, cols]
        q_t, do_t = q.T, do.T
        lse, delta = lse_ref[h : h + 1, :], delta_ref[h : h + 1, :]
        acc = jnp.zeros((HEAD_DIM, BLOCK), f32)
        for part in range(2):
            rows = slice(part * HALF, (part + 1) * HALF)
            dk, dv, dq = step(
                pkv_ref[rows, cols], pkv_ref[rows, vcols], q, do, q_t, do_t, delta,
                lambda p: p * SCORE_SCALE + (prev_bias - lse),
            )
            rim_ref[rows, cols] = dk.astype(bf16)
            rim_ref[rows, vcols] = dv.astype(bf16)
            acc = acc + dq
        dq_ref[cols, :] = acc


def near_kernel(q_ref, kv_ref, lse_ref, do_ref, delta_ref, dq_in, dq_ref, near_ref):
    for h in range(HEADS_DEV):
        cols, vcols = head_cols(h)
        q, do = q_ref[:, cols], do_ref[:, cols]
        q_t, do_t = q.T, do.T
        lse, delta = lse_ref[h : h + 1, :], delta_ref[h : h + 1, :]
        acc = dq_in[cols, :]
        for part in range(2):
            rows = slice(part * HALF, (part + 1) * HALF)
            dk, dv, dq = step(
                kv_ref[rows, cols], kv_ref[rows, vcols], q, do, q_t, do_t, delta,
                lambda p: jnp.where(own_mask(part * HALF), p * SCORE_SCALE - lse, NEGATIVE),
            )
            near_ref[rows, cols] = dk
            near_ref[rows, vcols] = dv
            acc = acc + dq
        dq_ref[:, cols] = (acc * SCALING).T.astype(bf16)


def core_kernel(own_ref, got_ref, *outs):
    def chunk(i):
        rows = slice(i * CHUNK, (i + 1) * CHUNK)
        return (wide(own_ref, rows) + wide(got_ref, rows)).astype(bf16)

    emit(chunk, outs)


def y_kernel(*refs):
    a, b = halves(*refs[:5])
    both = [h[i * MIDS : (i + 1) * MIDS] for h in (a, b) for i in range(2)]
    for out, chunk in zip(refs[5:], both):
        out[...] = chunk.astype(out.dtype)


def total(refs, rows):
    return sum((wide(ref, rows) for ref in refs[1:]), wide(refs[0], rows))


def x_kernel(own, got_behind, got_ahead, last_behind, last_ahead, keep_ref, pass_ref):
    a, b = halves(own, got_behind, got_ahead, last_behind, last_ahead)
    keep_ref[...] = a
    pass_ref[...] = b.astype(bf16)


def pair_kernel(keep_ref, got_ref, out_ref):
    out_ref[...] = (keep_ref[...] + got_ref[...].astype(f32)).astype(bf16)


def last_kernel(*refs):
    near_ref, rim_ref, key_ref, value_ref, weight_ref = refs[Z:]
    sums = total(refs[:Z], slice(0, MIDS))
    weight_ref[...] = sums[:, 2 * COLS :]
    mid = sums[:, : 2 * COLS] * (1.0 / POOL_MID)
    spread = jnp.broadcast_to(mid[:, None, :], (MIDS, POOL_MID, 2 * COLS)).reshape(BLOCK, 2 * COLS)
    grad = near_ref[...] + rim_ref[...].astype(f32) + spread
    key_ref[...] = grad[:, :COLS].astype(bf16)
    value_ref[...] = grad[:, COLS:].astype(bf16)


def on_device(queries, key_frames, value_frames, out_weight, out_grad, near_window, mid_start):
    dma = pltpu.SemaphoreType.DMA
    smem_window = pltpu.SMEM((Z * Y * C,), jnp.int32)
    smem_bias = pltpu.SMEM(((Y + 1) * Z,), f32)
    vmem_scores = pltpu.VMEM((BLOCK + (Y + 1) * CHUNK, BLOCK), f32)
    grad_t = shape(COLS, BLOCK, dtype=f32)
    rows_t = shape(HEADS_DEV, BLOCK, dtype=f32)
    half_rows = FAR_KEYS // 2
    pair_flops = 2 * HEADS_DEV * BLOCK * HEAD_DIM

    kv = jnp.concatenate([key_frames, value_frames], axis=1)
    (mid,) = call(pool_kernel, [shape(MIDS, 2 * COLS)])(kv)
    pair = along_head(out_grad, dz=1)
    run, grads = call(gather_kernel, [shape(CHUNK, 2 * COLS), shape(2 * BLOCK, COLS)])(
        mid, *[along_z(mid, i) for i in range(1, Z)], out_grad, pair
    )
    ahead, behind = along_y(run, 1), along_y(run, -1)
    ahead_g, behind_g = along_x(grads, 1), along_x(grads, -1)
    first, rest, three, keys = call(
        part_kernel,
        [shape(CHUNK // 2, 2 * COLS)] * 2 + [shape(3 * CHUNK, 2 * COLS), shape(BLOCK, COLS)],
    )(run, ahead, behind, kv)
    prev_keys, prev_values = passed_along(keys, 1), passed_along(value_frames, 1)
    three_other = along_seq(three, dc=1)
    scratch = [vmem_scores, smem_window, smem_window, smem_bias, dma((2,))]
    far_three, top, sums, out = call(
        first_kernel,
        [shape(3 * CHUNK, 2 * COLS), rows_t, rows_t, grad_t],
        scratch,
        far=2,
        flops=4 * pair_flops * 1536,
        count=2 * BLOCK * 1536,
    )(near_window, mid_start, queries, kv, three)
    last, *beyond = call(
        join_kernel,
        [shape(CHUNK, 2 * COLS), shape(BLOCK, COLS), shape(BLOCK, COLS)],
        after=(prev_keys, top),
    )(along_y(first, 1), along_y(rest, -1), ahead_g, behind_g)
    last_other = along_seq(last, dc=1)
    grads = [grads, ahead_g, along_x(beyond[0], 1), along_x(beyond[1], -1), behind_g]

    far_own, far_other, prev_kv, attention, lse, *parts = call(
        second_kernel,
        [
            shape(half_rows, 2 * COLS),
            shape(half_rows, 2 * COLS),
            shape(BLOCK, 2 * COLS),
            shape(BLOCK, COLS),
            rows_t,
            *ring_shapes(2 * BLOCK, COLS),
        ],
        scratch,
        far=2,
        flops=4 * pair_flops * 1536 + 2 * BLOCK * 2048 * COLS,
        count=2 * BLOCK * 1536,
    )(
        near_window, mid_start, queries, out_weight, prev_keys, prev_values, last, three_other,
        last_other, far_three, top, sums, out,
    )

    attention_grad, delta, weight_own, weight_other = call(
        project_kernel,
        [shape(BLOCK, COLS), rows_t, shape(half_rows, COLS), shape(half_rows, COLS)],
        flops=4 * BLOCK * 2048 * COLS,
    )(out_weight, attention, *grads)
    rim, dq = call(
        prev_kernel,
        [shape(BLOCK, 2 * COLS), grad_t],
        [smem_window, dma((1,))],
        far=1,
        flops=10 * pair_flops * 512,
        count=2 * BLOCK * 512,
    )(near_window, queries, prev_kv, lse, attention_grad, delta)
    rim_got = passed_along(rim, -1)

    def far_grads(first, far, weight, dq):
        return call(
            functools.partial(far_kernel, first),
            [shape(half_rows, SUM_COLS), grad_t],
            [smem_window, smem_bias, dma((1,))],
            far=1,
            flops=10 * pair_flops * 1024,
            count=2 * BLOCK * 1024,
        )(near_window, queries, far, lse, attention_grad, delta, dq, weight)

    sums_other, dq = far_grads(Y, far_other, weight_other, dq)
    sums_got = along_seq(sums_other, dc=1)
    sums_own, dq = far_grads(0, far_own, weight_own, dq)
    sums = call(core_kernel, ring_shapes(CHUNK, SUM_COLS))(sums_own, sums_got)
    query_grad, near_grad = call(
        near_kernel,
        [shape(BLOCK, COLS), shape(BLOCK, 2 * COLS, dtype=f32)],
        flops=10 * pair_flops * 512,
        count=2 * BLOCK * 512,
        after=(sums[0], rim_got),
    )(queries, kv, lse, attention_grad, delta, dq)

    parts, _ = ring(parts, along_x, after=(near_grad,))
    sums, turned = ring(sums, along_y, after=(near_grad,))
    keep, given = call(
        x_kernel, [shape(BLOCK, COLS, dtype=f32), shape(BLOCK, COLS)], after=(turned,)
    )(*parts)
    given = along_head(given, dz=1)
    sums = call(y_kernel, [shape(MIDS, SUM_COLS, dtype=f32)] + [shape(MIDS, SUM_COLS)] * 3)(*sums)
    sums = [sums[0]] + [along_z(sums[i], -i) for i in range(1, Z)]
    (layer_out,) = call(pair_kernel, [shape(BLOCK, COLS)])(keep, given)
    key_grad, value_grad, weight_t = call(
        last_kernel,
        [shape(BLOCK, COLS), shape(BLOCK, COLS), shape(MIDS, COLS, dtype=f32)],
    )(*sums, near_grad, rim_got)
    return layer_out, query_grad, key_grad, value_grad, weight_t.T


def solution(mesh):
    return jax.shard_map(
        on_device,
        mesh=mesh,
        in_specs=(
            P("seq", "head"),
            P("seq", "head"),
            P("seq", "head"),
            P("head", None),
            P("seq", "head"),
            P(),
            P(),
        ),
        out_specs=(
            P("seq", "head"),
            P("seq", "head"),
            P("seq", "head"),
            P("seq", "head"),
            P("head", "seq"),
        ),
        check_vma=False,
    )
```

time: 121 us -> 119 us (0.983)
  waiting for transfers between devices: 42.4 us -> 39.4 us
  starting transfers between devices: 48.4 us -> 51.2 us
    ppermute x12 -> x10, waiting for transfers between devices: 10.5 us -> 5.82 us  [along_head(): return lax.ppermute(value, 'head', pairs)]
    ppermute x19 -> x17, starting transfers between devices: 28.4 us -> 32.8 us  [along_seq(): return lax.ppermute(value, 'seq', pairs)]
    ppermute x12 -> x10, starting transfers between devices: 16.6 us -> 13.5 us  [along_head(): return lax.ppermute(value, 'head', pairs)]
    ppermute x19 -> x17, waiting for transfers between devices: 31.8 us -> 33.5 us  [along_seq(): return lax.ppermute(value, 'seq', pairs)]
    ppermute x2 -> x3, starting transfers between devices: 3.36 us -> 4.9 us  [passed_along(): lax.ppermute(value, 'seq', [(source, source + steps) for source in range(...]
    pallas_call x16 -> x18, Pallas kernels: 26.5 us -> 25.7 us  [run(): pl.pallas_call(body, out_shape=list(outs), in_specs=[pl.BlockSpec(memory_...]
  transfers between devices with their start and end apart: 33 -> 30, of which waited for: 16 -> 15; matrix products, arithmetic and copies ran while one was open for 0% -> 2% of each run, Pallas kernels for 16% -> 13%
where the time goes in v1:
time: 119 us
  starting transfers between devices  51.2 us (43%)
  waiting for transfers between devices  39.4 us (33%)
  Pallas kernels  25.7 us (22%)
  local copies, waits for them, and re-layouts  2.01 us (2%)
    ppermute x17, waiting for transfers between devices, along_seq(): return lax.ppermute(value, 'seq', pairs)  33.5 us
    ppermute x17, starting transfers between devices, along_seq(): return lax.ppermute(value, 'seq', pairs)  32.8 us
    pallas_call x18, Pallas kernels, run(): pl.pallas_call(body, out_shape=list(outs), in_specs=[pl.BlockSpec(memory_...  25.7 us
    ppermute x10, starting transfers between devices, along_head(): return lax.ppermute(value, 'head', pairs)  13.5 us
    ppermute x10, waiting for transfers between devices, along_head(): return lax.ppermute(value, 'head', pairs)  5.82 us
    ppermute x3, starting transfers between devices, passed_along(): lax.ppermute(value, 'seq', [(source, source + steps) for source in range(...  4.9 us
  transfers between devices with their start and end apart: 30, of which 15 were waited for; matrix products, arithmetic and copies ran while one was open for 2% of the time, Pallas kernels for 13%

profile of v1, /device:TPU:32, one launch (start us, length us, event | category | flops | bytes accessed | tf_op | source)
XLA Modules:
  0.0 119.2 jit_solution(12835703739063998833)
XLA Ops:
  4.8 4.6 %collective-permute-start.2 = (bf16[64,512]{1,0:T(8,128)(2,1)S(1)}, bf16[64,512]{1,0:T(8,128)(2,1)S(1)}, u32[]{:S(2)}, u32[]{:S(2)}) collective-permute-start(bf16[64,512]{1,0:T(8,128)(2,1)S(1)} %shard_map.110.refs_0_), channel_id=1, source_target_pairs={{0,192},{8,200},{16,208},{24,216},{32,224},{40,232},{48,240},{56,2... | collective-permute-start | bytes 196616 | tf_op jit(solution)/shard_map/ppermute | solution.py:41
  10.4 2.8 %collective-permute-start = (bf16[64,512]{1,0:T(8,128)(2,1)S(1)}, bf16[64,512]{1,0:T(8,128)(2,1)S(1)}, u32[]{:S(2)}, u32[]{:S(2)}) collective-permute-start(bf16[64,512]{1,0:T(8,128)(2,1)S(1)} %shard_map.110.refs_0_), channel_id=1, source_target_pairs={{0,64},{8,72},{16,80},{24,88},{32,96},{40,104},{48,112},{56,120},{... | collective-permute-start | bytes 196616 | tf_op jit(solution)/shard_map/ppermute | solution.py:41
  13.5 5.6 %collective-permute-done.1.refs_2_ = bf16[64,512]{1,0:T(8,128)(2,1)S(1)} collective-permute-done((bf16[64,512]{1,0:T(8,128)(2,1)S(1)}, bf16[64,512]{1,0:T(8,128)(2,1)S(1)}, u32[]{:S(2)}, u32[]{:S(2)}) %collective-permute-start.1) | collective-permute-done | bytes 65568 | tf_op jit(solution)/shard_map/ppermute | solution.py:41
  19.4 3.1 %collective-permute-start.5 = (bf16[256,512]{1,0:T(8,128)(2,1)S(1)}, bf16[256,512]{1,0:T(8,128)(2,1)S(1)}, u32[]{:S(2)}, u32[]{:S(2)}) collective-permute-start(bf16[256,512]{1,0:T(8,128)(2,1)S(1)} %get-tuple-element.58.refs_0_), channel_id=1, source_target_pairs={{0,48},{8,56},{16,0},{24,8},{32,16},{40,24},{48,32},{56,40},{64,11... | collective-permute-start | bytes 786440 | tf_op jit(solution)/shard_map/ppermute | solution.py:41
  22.5 2.8 %collective-permute-start.11 = (bf16[1024,256]{1,0:T(8,128)(2,1)S(1)}, bf16[1024,256]{1,0:T(8,128)(2,1)S(1)}, u32[]{:S(2)}, u32[]{:S(2)}) collective-permute-start(bf16[1024,256]{1,0:T(8,128)(2,1)S(1)} %get-tuple-element.62.refs_2_), channel_id=1, source_target_pairs={{0,3},{1,0},{2,1},{3,2},{4,7},{5,4},{6,5},{7,6},{8,11},{9,8},{10,9... | collective-permute-start | bytes 1572872 | tf_op jit(solution)/shard_map/ppermute | solution.py:49
  26.4 3.7 %collective-permute-done.4.refs_1_ = bf16[256,512]{1,0:T(8,128)(2,1)S(1)} collective-permute-done((bf16[256,512]{1,0:T(8,128)(2,1)S(1)}, bf16[256,512]{1,0:T(8,128)(2,1)S(1)}, u32[]{:S(2)}, u32[]{:S(2)}) %collective-permute-start.4) | collective-permute-done | bytes 262176 | tf_op jit(solution)/shard_map/ppermute | solution.py:41
  30.3 2.3 %collective-permute-start.6 = (bf16[512,256]{1,0:T(8,128)(2,1)S(1)}, bf16[512,256]{1,0:T(8,128)(2,1)S(1)}, u32[]{:S(2)}, u32[]{:S(2)}) collective-permute-start(bf16[512,256]{1,0:T(8,128)(2,1)S(1)} %get-tuple-element.59), channel_id=1, source_target_pairs={{0,8},{8,16},{16,24},{24,32},{32,40},{40,48},{48,56},{56,64},{64,7... | collective-permute-start | bytes 786440 | tf_op jit(solution)/shard_map/ppermute | solution.py:67
  32.7 4.7 %collective-permute-done.8.refs_0_ = bf16[128,512]{1,0:T(8,128)(2,1)S(1)} collective-permute-done((bf16[128,512]{1,0:T(8,128)(2,1)S(1)}, bf16[128,512]{1,0:T(8,128)(2,1)S(1)}, u32[]{:S(2)}, u32[]{:S(2)}) %collective-permute-start.8) | collective-permute-done | bytes 131104 | tf_op jit(solution)/shard_map/ppermute | solution.py:41
  37.4 3.0 %shard_map.113 = (bf16[768,512]{1,0:T(8,128)(2,1)S(1)}, f32[2,512]{1,0:T(2,128)S(1)}, f32[2,512]{1,0:T(2,128)S(1)}, f32[256,512]{1,0:T(8,128)S(1)}) custom-call(s32[32]{0:T(128)S(1)} %copy-done.4, s32[32]{0:T(128)S(1)} %copy-done.3, bf16[512,256]{1,0:T(8,128)(2,1)S(1)} %copy-done.2, ...), custom_call_target="tpu_custom_call" | custom-call | flops 1610612736 | bytes 2892032 | tf_op jit(solution)/shard_map/pallas_call | solution.py:81
  48.0 4.7 %shard_map.115 = (bf16[1024,512]{1,0:T(8,128)(2,1)S(1)}, bf16[1024,512]{1,0:T(8,128)(2,1)S(1)}, bf16[512,512]{1,0:T(8,128)(2,1)S(1)}, bf16[512,256]{1,0:T(8,128)...) custom-call(s32[32]{0:T(128)S(1)} %copy-done.4, ...), custom_call_target="tpu_custom_call" | custom-call | flops 2147483648 | bytes 9449728 | tf_op jit(solution)/shard_map/pallas_call | solution.py:81
  54.3 3.0 %shard_map.116 = (bf16[512,256]{1,0:T(8,128)(2,1)S(1)}, f32[2,512]{1,0:T(2,128)S(1)}, bf16[1024,256]{1,0:T(8,128)(2,1)S(1)}, bf16[1024,256]{1,0:T(8,128)(2,1)S(1)}) custom-call(bf16[256,2048]{1,0:T(8,128)(2,1)S(1)} %copy-done.1, bf16[512,256]{1,0:T(8,128)(2,1)S(1)} %get-tuple-element.75.refs_1_, bf16[1024,256]{1,0:T(8,128)(2,1)S(1)} %get-tuple-element.62.refs_2_, ...), custom_call_target="tpu_custom_call" | custom-call | flops 1073741824 | bytes 4722688 | tf_op jit(solution)/shard_map/pallas_call | solution.py:81
  59.3 3.9 %shard_map.118 = (bf16[1024,768]{1,0:T(8,128)(2,1)S(1)}, f32[256,512]{1,0:T(8,128)S(1)}) custom-call(s32[32]{0:T(128)S(1)} %copy-done.4, bf16[512,256]{1,0:T(8,128)(2,1)S(1)} %copy-done.2, bf16[1024,512]{1,0:T(8,128)(2,1)S(1)} %get-tuple-element.81.refs_2_, f32[2,512]{1,0:T(2,128)S(1)} %get-tuple-element.74.refs_3_.refs_2_, ...), custom_call_target="tpu_custom_call" | custom-call | flops 2684354560 | bytes 4726912 | tf_op jit(solution)/shard_map/pallas_call | solution.py:81
  64.6 3.1 %collective-permute-start.14 = (bf16[1024,256]{1,0:T(8,128)(2,1)S(1)}, bf16[1024,256]{1,0:T(8,128)(2,1)S(1)}, u32[]{:S(2)}, u32[]{:S(2)}) collective-permute-start(bf16[1024,256]{1,0:T(8,128)(2,1)S(1)} %get-tuple-element.70), channel_id=1, source_target_pairs={{0,3},{1,0},{2,1},{3,2},{4,7},{5,4},{6,5},{7,6},{8,11},{9,8},{10,9... | collective-permute-start | bytes 1572872 | tf_op jit(solution)/shard_map/ppermute | solution.py:49
  67.7 3.9 %shard_map.119 = (bf16[1024,768]{1,0:T(8,128)(2,1)S(1)}, f32[256,512]{1,0:T(8,128)S(1)}) custom-call(s32[32]{0:T(128)S(1)} %copy-done.4, bf16[512,256]{1,0:T(8,128)(2,1)S(1)} %copy-done.2, bf16[1024,512]{1,0:T(8,128)(2,1)S(1)} %get-tuple-element.80.refs_2_, f32[2,512]{1,0:T(2,128)S(1)} %get-tuple-element.74.refs_3_.refs_2_, ...), custom_call_target="tpu_custom_call" | custom-call | flops 2684354560 | bytes 4726912 | tf_op jit(solution)/shard_map/pallas_call | solution.py:81
  71.9 2.8 %collective-permute-start.23 = (bf16[256,768]{1,0:T(8,128)(2,1)S(1)}, bf16[256,768]{1,0:T(8,128)(2,1)S(1)}, u32[]{:S(2)}, u32[]{:S(2)}) collective-permute-start(bf16[256,768]{1,0:T(8,128)(2,1)S(1)} %get-tuple-element.97), channel_id=1, source_target_pairs={{0,16},{8,24},{16,32},{24,40},{32,48},{40,56},{48,0},{56,8},{64,80... | collective-permute-start | bytes 1179656 | tf_op jit(solution)/shard_map/ppermute | solution.py:41
  74.7 2.9 %collective-permute-start.22 = (bf16[256,768]{1,0:T(8,128)(2,1)S(1)}, bf16[256,768]{1,0:T(8,128)(2,1)S(1)}, u32[]{:S(2)}, u32[]{:S(2)}) collective-permute-start(bf16[256,768]{1,0:T(8,128)(2,1)S(1)} %get-tuple-element.90.refs_6_), channel_id=1, source_target_pairs={{0,48},{8,56},{16,0},{24,8},{32,16},{40,24},{48,32},{56,40},{64,11... | collective-permute-start | bytes 1179656 | tf_op jit(solution)/shard_map/ppermute | solution.py:41
  77.7 2.2 %shard_map.121 = (bf16[512,256]{1,0:T(8,128)(2,1)}, f32[512,512]{1,0:T(8,128)S(1)}) custom-call(bf16[512,256]{1,0:T(8,128)(2,1)S(1)} %copy-done.2, bf16[512,512]{1,0:T(8,128)(2,1)S(1)} %constant_dynamic-update-slice_fusion.refs_0_.refs_3_.refs_1_, f32[2,512]{1,0:T(2,128)S(1)} %get-tuple-element.74.refs_3_.refs_2_, ...), custom_call_target="tpu_custom_call" | custom-call | flops 1342177280 | bytes 2891776 | tf_op jit(solution)/shard_map/pallas_call | solution.py:81
  79.9 3.7 %collective-permute-done.15.refs_3_.refs_2_ = bf16[1024,256]{1,0:T(8,128)(2,1)S(1)} collective-permute-done((bf16[1024,256]{1,0:T(8,128)(2,1)S(1)}, bf16[1024,256]{1,0:T(8,128)(2,1)S(1)}, u32[]{:S(2)}, u32[]{:S(2)}) %collective-permute-start.15) | collective-permute-done | bytes 524320 | tf_op jit(solution)/shard_map/ppermute | solution.py:49
  88.9 3.8 %collective-permute-start.25 = (bf16[128,768]{1,0:T(8,128)(2,1)S(1)}, bf16[128,768]{1,0:T(8,128)(2,1)S(1)}, u32[]{:S(2)}, u32[]{:S(2)}) collective-permute-start(bf16[128,768]{1,0:T(8,128)(2,1)S(1)} %get-tuple-element.98.refs_5_), channel_id=1, source_target_pairs={{0,48},{8,56},{16,0},{24,8},{32,16},{40,24},{48,32},{56,40},{64,11... | collective-permute-start | bytes 589832 | tf_op jit(solution)/shard_map/ppermute | solution.py:41
  93.9 3.8 %collective-permute-done.26.refs_4_ = bf16[128,768]{1,0:T(8,128)(2,1)S(1)} collective-permute-done((bf16[128,768]{1,0:T(8,128)(2,1)S(1)}, bf16[128,768]{1,0:T(8,128)(2,1)S(1)}, u32[]{:S(2)}, u32[]{:S(2)}) %collective-permute-start.26) | collective-permute-done | bytes 196640 | tf_op jit(solution)/shard_map/ppermute | solution.py:41
  97.8 2.9 %collective-permute-start.27 = (bf16[64,768]{1,0:T(8,128)(2,1)S(1)}, bf16[64,768]{1,0:T(8,128)(2,1)S(1)}, u32[]{:S(2)}, u32[]{:S(2)}) collective-permute-start(bf16[64,768]{1,0:T(8,128)(2,1)S(1)} %get-tuple-element.105), channel_id=1, source_target_pairs={{0,192},{8,200},{16,208},{24,216},{32,224},{40,232},{48,240},{56,2... | collective-permute-start | bytes 294920 | tf_op jit(solution)/shard_map/ppermute | solution.py:41
  100.7 4.7 %collective-permute-start.28 = (bf16[64,768]{1,0:T(8,128)(2,1)S(1)}, bf16[64,768]{1,0:T(8,128)(2,1)S(1)}, u32[]{:S(2)}, u32[]{:S(2)}) collective-permute-start(bf16[64,768]{1,0:T(8,128)(2,1)S(1)} %get-tuple-element.106), channel_id=1, source_target_pairs={{0,128},{8,136},{16,144},{24,152},{32,160},{40,168},{48,176},{56,1... | collective-permute-start | bytes 294920 | tf_op jit(solution)/shard_map/ppermute | solution.py:41
  105.4 2.8 %collective-permute-start.29 = (bf16[64,768]{1,0:T(8,128)(2,1)S(1)}, bf16[64,768]{1,0:T(8,128)(2,1)S(1)}, u32[]{:S(2)}, u32[]{:S(2)}) collective-permute-start(bf16[64,768]{1,0:T(8,128)(2,1)S(1)} %get-tuple-element.107), channel_id=1, source_target_pairs={{0,64},{8,72},{16,80},{24,88},{32,96},{40,104},{48,112},{56,120},{... | collective-permute-start | bytes 294920 | tf_op jit(solution)/shard_map/ppermute | solution.py:41
  111.2 7.0 %collective-permute-done.28.refs_2_ = bf16[64,768]{1,0:T(8,128)(2,1)S(1)} collective-permute-done((bf16[64,768]{1,0:T(8,128)(2,1)S(1)}, bf16[64,768]{1,0:T(8,128)(2,1)S(1)}, u32[]{:S(2)}, u32[]{:S(2)}) %collective-permute-start.28) | collective-permute-done | bytes 98336 | tf_op jit(solution)/shard_map/ppermute | solution.py:41
  (68 shorter events, 30.3 us)
Async XLA Ops:
  0.6 18.7 %collective-permute-start.3 = (bf16[512,256]{1,0:T(8,128)(2,1)}, bf16[512,256]{1,0:T(8,128)(2,1)S(1)}, u32[]{:S(2)}, u32[]{:S(2)}) collective-permute-start(bf16[512,256]{1,0:T(8,128)(2,1)} %refs_4_.1), channel_id=1, source_target_pairs={{0,4},{1,5},{2,6},{3,7},{4,0},{5,1},{6,2},{7,3},{8,12},{9,13},{10,... | collective-permute-start | bytes 786440 | tf_op jit(solution)/shard_map/ppermute | solution.py:49
  4.8 8.7 %collective-permute-start.2 = (bf16[64,512]{1,0:T(8,128)(2,1)S(1)}, bf16[64,512]{1,0:T(8,128)(2,1)S(1)}, u32[]{:S(2)}, u32[]{:S(2)}) collective-permute-start(bf16[64,512]{1,0:T(8,128)(2,1)S(1)} %shard_map.110.refs_0_), channel_id=1, source_target_pairs={{0,192},{8,200},{16,208},{24,216},{32,224},{40,232},{48,240},{56,2... | collective-permute-start | bytes 196616 | tf_op jit(solution)/shard_map/ppermute | solution.py:41
  9.4 9.7 %collective-permute-start.1 = (bf16[64,512]{1,0:T(8,128)(2,1)S(1)}, bf16[64,512]{1,0:T(8,128)(2,1)S(1)}, u32[]{:S(2)}, u32[]{:S(2)}) collective-permute-start(bf16[64,512]{1,0:T(8,128)(2,1)S(1)} %shard_map.110.refs_0_), channel_id=1, source_target_pairs={{0,128},{8,136},{16,144},{24,152},{32,160},{40,168},{48,176},{56,1... | collective-permute-start | bytes 196616 | tf_op jit(solution)/shard_map/ppermute | solution.py:41
  10.4 8.9 %collective-permute-start = (bf16[64,512]{1,0:T(8,128)(2,1)S(1)}, bf16[64,512]{1,0:T(8,128)(2,1)S(1)}, u32[]{:S(2)}, u32[]{:S(2)}) collective-permute-start(bf16[64,512]{1,0:T(8,128)(2,1)S(1)} %shard_map.110.refs_0_), channel_id=1, source_target_pairs={{0,64},{8,72},{16,80},{24,88},{32,96},{40,104},{48,112},{56,120},{... | collective-permute-start | bytes 196616 | tf_op jit(solution)/shard_map/ppermute | solution.py:41
  22.5 21.3 %collective-permute-start.11 = (bf16[1024,256]{1,0:T(8,128)(2,1)S(1)}, bf16[1024,256]{1,0:T(8,128)(2,1)S(1)}, u32[]{:S(2)}, u32[]{:S(2)}) collective-permute-start(bf16[1024,256]{1,0:T(8,128)(2,1)S(1)} %get-tuple-element.62.refs_2_), channel_id=1, source_target_pairs={{0,3},{1,0},{2,1},{3,2},{4,7},{5,4},{6,5},{7,6},{8,11},{9,8},{10,9... | collective-permute-start | bytes 1572872 | tf_op jit(solution)/shard_map/ppermute | solution.py:49
  25.2 18.5 %collective-permute-start.10 = (bf16[1024,256]{1,0:T(8,128)(2,1)S(1)}, bf16[1024,256]{1,0:T(8,128)(2,1)S(1)}, u32[]{:S(2)}, u32[]{:S(2)}) collective-permute-start(bf16[1024,256]{1,0:T(8,128)(2,1)S(1)} %get-tuple-element.62.refs_2_), channel_id=1, source_target_pairs={{0,1},{1,2},{2,3},{3,0},{4,5},{5,6},{6,7},{7,4},{8,9},{9,10},{10,1... | collective-permute-start | bytes 1572872 | tf_op jit(solution)/shard_map/ppermute | solution.py:49
  30.2 17.8 %collective-permute-start.12 = (bf16[768,512]{1,0:T(8,128)(2,1)S(1)}, bf16[768,512]{1,0:T(8,128)(2,1)S(1)}, u32[]{:S(2)}, u32[]{:S(2)}) collective-permute-start(bf16[768,512]{1,0:T(8,128)(2,1)S(1)} %get-tuple-element.63.refs_4_), channel_id=1, source_target_pairs={{0,8},{8,0},{16,24},{24,16},{32,40},{40,32},{48,56},{56,48},{64,72... | collective-permute-start | bytes 2359304 | tf_op jit(solution)/shard_map/ppermute | solution.py:41
  30.3 13.4 %collective-permute-start.6 = (bf16[512,256]{1,0:T(8,128)(2,1)S(1)}, bf16[512,256]{1,0:T(8,128)(2,1)S(1)}, u32[]{:S(2)}, u32[]{:S(2)}) collective-permute-start(bf16[512,256]{1,0:T(8,128)(2,1)S(1)} %get-tuple-element.59), channel_id=1, source_target_pairs={{0,8},{8,16},{16,24},{24,32},{32,40},{40,48},{48,56},{56,64},{64,7... | collective-permute-start | bytes 786440 | tf_op jit(solution)/shard_map/ppermute | solution.py:67
  44.7 9.5 %collective-permute-start.16 = (bf16[512,256]{1,0:T(8,128)(2,1)S(1)}, bf16[512,256]{1,0:T(8,128)(2,1)S(1)}, u32[]{:S(2)}, u32[]{:S(2)}) collective-permute-start(bf16[512,256]{1,0:T(8,128)(2,1)S(1)} %get-tuple-element.76), channel_id=1, source_target_pairs={{0,1},{1,2},{2,3},{3,0},{4,5},{5,6},{6,7},{7,4},{8,9},{9,10},{10,1... | collective-permute-start | bytes 786440 | tf_op jit(solution)/shard_map/ppermute | solution.py:49
  46.2 8.0 %collective-permute-start.17 = (bf16[512,256]{1,0:T(8,128)(2,1)S(1)}, bf16[512,256]{1,0:T(8,128)(2,1)S(1)}, u32[]{:S(2)}, u32[]{:S(2)}) collective-permute-start(bf16[512,256]{1,0:T(8,128)(2,1)S(1)} %get-tuple-element.77), channel_id=1, source_target_pairs={{0,3},{1,0},{2,1},{3,2},{4,7},{5,4},{6,5},{7,6},{8,11},{9,8},{10,9... | collective-permute-start | bytes 786440 | tf_op jit(solution)/shard_map/ppermute | solution.py:49
  63.2 8.4 %collective-permute-start.18 = (bf16[1024,768]{1,0:T(8,128)(2,1)S(1)}, bf16[1024,768]{1,0:T(8,128)(2,1)S(1)}, u32[]{:S(2)}, u32[]{:S(2)}) collective-permute-start(bf16[1024,768]{1,0:T(8,128)(2,1)S(1)} %get-tuple-element.89), channel_id=1, source_target_pairs={{0,8},{8,0},{16,24},{24,16},{32,40},{40,32},{48,56},{56,48},{64,72... | collective-permute-start | bytes 4718600 | tf_op jit(solution)/shard_map/ppermute | solution.py:41
  63.3 14.4 %collective-permute-start.19 = (bf16[512,512]{1,0:T(8,128)(2,1)S(1)}, bf16[512,512]{1,0:T(8,128)(2,1)S(1)}, u32[]{:S(2)}, u32[]{:S(2)}) collective-permute-start(bf16[512,512]{1,0:T(8,128)(2,1)S(1)} %get-tuple-element.91), channel_id=1, source_target_pairs={{8,0},{16,8},{24,16},{32,24},{40,32},{48,40},{56,48},{64,56},{72,6... | collective-permute-start | bytes 1572872 | tf_op jit(solution)/shard_map/ppermute | solution.py:67
  64.6 15.3 %collective-permute-start.14 = (bf16[1024,256]{1,0:T(8,128)(2,1)S(1)}, bf16[1024,256]{1,0:T(8,128)(2,1)S(1)}, u32[]{:S(2)}, u32[]{:S(2)}) collective-permute-start(bf16[1024,256]{1,0:T(8,128)(2,1)S(1)} %get-tuple-element.70), channel_id=1, source_target_pairs={{0,3},{1,0},{2,1},{3,2},{4,7},{5,4},{6,5},{7,6},{8,11},{9,8},{10,9... | collective-permute-start | bytes 1572872 | tf_op jit(solution)/shard_map/ppermute | solution.py:49
  67.7 15.9 %collective-permute-start.15 = (bf16[1024,256]{1,0:T(8,128)(2,1)S(1)}, bf16[1024,256]{1,0:T(8,128)(2,1)S(1)}, u32[]{:S(2)}, u32[]{:S(2)}) collective-permute-start(bf16[1024,256]{1,0:T(8,128)(2,1)S(1)} %get-tuple-element.71), channel_id=1, source_target_pairs={{0,1},{1,2},{2,3},{3,0},{4,5},{5,6},{6,7},{7,4},{8,9},{9,10},{10,1... | collective-permute-start | bytes 1572872 | tf_op jit(solution)/shard_map/ppermute | solution.py:49
  71.9 15.2 %collective-permute-start.23 = (bf16[256,768]{1,0:T(8,128)(2,1)S(1)}, bf16[256,768]{1,0:T(8,128)(2,1)S(1)}, u32[]{:S(2)}, u32[]{:S(2)}) collective-permute-start(bf16[256,768]{1,0:T(8,128)(2,1)S(1)} %get-tuple-element.97), channel_id=1, source_target_pairs={{0,16},{8,24},{16,32},{24,40},{32,48},{40,56},{48,0},{56,8},{64,80... | collective-permute-start | bytes 1179656 | tf_op jit(solution)/shard_map/ppermute | solution.py:41
  74.7 13.9 %collective-permute-start.22 = (bf16[256,768]{1,0:T(8,128)(2,1)S(1)}, bf16[256,768]{1,0:T(8,128)(2,1)S(1)}, u32[]{:S(2)}, u32[]{:S(2)}) collective-permute-start(bf16[256,768]{1,0:T(8,128)(2,1)S(1)} %get-tuple-element.90.refs_6_), channel_id=1, source_target_pairs={{0,48},{8,56},{16,0},{24,8},{32,16},{40,24},{48,32},{56,40},{64,11... | collective-permute-start | bytes 1179656 | tf_op jit(solution)/shard_map/ppermute | solution.py:41
  83.7 9.0 %collective-permute-start.20 = (bf16[512,256]{1,0:T(8,128)(2,1)S(1)}, bf16[512,256]{1,0:T(8,128)(2,1)S(1)}, u32[]{:S(2)}, u32[]{:S(2)}) collective-permute-start(bf16[512,256]{1,0:T(8,128)(2,1)S(1)} %get-tuple-element.93), channel_id=1, source_target_pairs={{0,3},{1,0},{2,1},{3,2},{4,7},{5,4},{6,5},{7,6},{8,11},{9,8},{10,9... | collective-permute-start | bytes 786440 | tf_op jit(solution)/shard_map/ppermute | solution.py:49
  83.8 9.5 %collective-permute-start.21 = (bf16[512,256]{1,0:T(8,128)(2,1)S(1)}, bf16[512,256]{1,0:T(8,128)(2,1)S(1)}, u32[]{:S(2)}, u32[]{:S(2)}) collective-permute-start(bf16[512,256]{1,0:T(8,128)(2,1)S(1)} %get-tuple-element.94), channel_id=1, source_target_pairs={{0,1},{1,2},{2,3},{3,0},{4,5},{5,6},{6,7},{7,4},{8,9},{9,10},{10,1... | collective-permute-start | bytes 786440 | tf_op jit(solution)/shard_map/ppermute | solution.py:49
  88.8 8.9 %collective-permute-start.26 = (bf16[128,768]{1,0:T(8,128)(2,1)S(1)}, bf16[128,768]{1,0:T(8,128)(2,1)S(1)}, u32[]{:S(2)}, u32[]{:S(2)}) collective-permute-start(bf16[128,768]{1,0:T(8,128)(2,1)S(1)} %get-tuple-element.103), channel_id=1, source_target_pairs={{0,16},{8,24},{16,32},{24,40},{32,48},{40,56},{48,0},{56,8},{64,80... | collective-permute-start | bytes 589832 | tf_op jit(solution)/shard_map/ppermute | solution.py:41
  88.9 8.8 %collective-permute-start.25 = (bf16[128,768]{1,0:T(8,128)(2,1)S(1)}, bf16[128,768]{1,0:T(8,128)(2,1)S(1)}, u32[]{:S(2)}, u32[]{:S(2)}) collective-permute-start(bf16[128,768]{1,0:T(8,128)(2,1)S(1)} %get-tuple-element.98.refs_5_), channel_id=1, source_target_pairs={{0,48},{8,56},{16,0},{24,8},{32,16},{40,24},{48,32},{56,40},{64,11... | collective-permute-start | bytes 589832 | tf_op jit(solution)/shard_map/ppermute | solution.py:41
  93.4 14.8 %collective-permute-start.24 = (bf16[512,256]{1,0:T(8,128)(2,1)S(1)}, bf16[512,256]{1,0:T(8,128)(2,1)S(1)}, u32[]{:S(2)}, u32[]{:S(2)}) collective-permute-start(bf16[512,256]{1,0:T(8,128)(2,1)S(1)} %get-tuple-element.100), channel_id=1, source_target_pairs={{0,4},{1,5},{2,6},{3,7},{4,0},{5,1},{6,2},{7,3},{8,12},{9,13},{10,... | collective-permute-start | bytes 786440 | tf_op jit(solution)/shard_map/ppermute | solution.py:49
  97.8 13.4 %collective-permute-start.27 = (bf16[64,768]{1,0:T(8,128)(2,1)S(1)}, bf16[64,768]{1,0:T(8,128)(2,1)S(1)}, u32[]{:S(2)}, u32[]{:S(2)}) collective-permute-start(bf16[64,768]{1,0:T(8,128)(2,1)S(1)} %get-tuple-element.105), channel_id=1, source_target_pairs={{0,192},{8,200},{16,208},{24,216},{32,224},{40,232},{48,240},{56,2... | collective-permute-start | bytes 294920 | tf_op jit(solution)/shard_map/ppermute | solution.py:41
  100.7 17.5 %collective-permute-start.28 = (bf16[64,768]{1,0:T(8,128)(2,1)S(1)}, bf16[64,768]{1,0:T(8,128)(2,1)S(1)}, u32[]{:S(2)}, u32[]{:S(2)}) collective-permute-start(bf16[64,768]{1,0:T(8,128)(2,1)S(1)} %get-tuple-element.106), channel_id=1, source_target_pairs={{0,128},{8,136},{16,144},{24,152},{32,160},{40,168},{48,176},{56,1... | collective-permute-start | bytes 294920 | tf_op jit(solution)/shard_map/ppermute | solution.py:41
  105.4 12.8 %collective-permute-start.29 = (bf16[64,768]{1,0:T(8,128)(2,1)S(1)}, bf16[64,768]{1,0:T(8,128)(2,1)S(1)}, u32[]{:S(2)}, u32[]{:S(2)}) collective-permute-start(bf16[64,768]{1,0:T(8,128)(2,1)S(1)} %get-tuple-element.107), channel_id=1, source_target_pairs={{0,64},{8,72},{16,80},{24,88},{32,96},{40,104},{48,112},{56,120},{... | collective-permute-start | bytes 294920 | tf_op jit(solution)/shard_map/ppermute | solution.py:41
  (12 other events, 169.3 us)

commit v2 on v1

--- a/solution.py
+++ b/solution.py
@@ -178,9 +178,11 @@
     keys_out[...] = kv_ref[:, :COLS]
 
 
-def join_kernel(first, rest, grads_1, grads_3, last_ref, own_out, pair_out):
-    last_ref[: CHUNK // 2] = first[...]
-    last_ref[CHUNK // 2 :] = rest[...]
+def join_kernel(three, first, rest, grads_1, grads_3, mids_ref, own_out, pair_out):
+    at = 0
+    for ref in (three, first, rest):
+        mids_ref[at : at + ref.shape[0]] = ref[...]
+        at += ref.shape[0]
     own_out[...] = grads_1[:BLOCK]
     pair_out[...] = grads_3[BLOCK:]
 
@@ -304,14 +306,13 @@
 
 
 def second_kernel(
-    nw_hbm, ms_hbm, q_ref, w_ref, pk_ref, pv_ref, last_ref, three_ref, other_ref, far_own_ref,
+    nw_hbm, ms_hbm, q_ref, w_ref, pk_ref, pv_ref, mids_ref, other_ref, far_own_ref,
     top_ref, sums_ref, out_ref, far_last_ref, far_ref, pkv_ref, att_ref, lse_ref, behind, ahead, late_behind, late_ahead, own,
     s_ref, nw_ref, ms_ref, bias_ref, sems,
 ):
     near_begin, mid_begin = window(nw_hbm, ms_hbm, nw_ref, ms_ref, sems)
-    chunks = [(0, 3, last_ref, 0, far_last_ref, 3 * CHUNK)]
-    chunks += [(1, i, three_ref, i * CHUNK, far_ref, i * CHUNK) for i in range(3)]
-    chunks += [(1, 3, other_ref, 0, far_ref, 3 * CHUNK)]
+    chunks = [(0, 3, mids_ref, 3 * CHUNK, far_last_ref, 3 * CHUNK)]
+    chunks += [(1, i, other_ref, i * CHUNK, far_ref, i * CHUNK) for i in range(Y)]
     effective(near_begin, mid_begin, chunks, bias_ref)
     far_last_ref[: 3 * CHUNK] = far_own_ref[...]
     pkv_ref[:, :COLS], pkv_ref[:, COLS:] = pk_ref[...], pv_ref[...]
@@ -536,7 +537,6 @@
         [shape(CHUNK // 2, 2 * COLS)] * 2 + [shape(3 * CHUNK, 2 * COLS), shape(BLOCK, COLS)],
     )(run, ahead, behind, kv)
     prev_keys, prev_values = passed_along(keys, 1), passed_along(value_frames, 1)
-    three_other = along_seq(three, dc=1)
     scratch = [vmem_scores, smem_window, smem_window, smem_bias, dma((2,))]
     far_three, top, sums, out = call(
         first_kernel,
@@ -546,12 +546,12 @@
         flops=4 * pair_flops * 1536,
         count=2 * BLOCK * 1536,
     )(near_window, mid_start, queries, kv, three)
-    last, *beyond = call(
+    mids_own, *beyond = call(
         join_kernel,
-        [shape(CHUNK, 2 * COLS), shape(BLOCK, COLS), shape(BLOCK, COLS)],
+        [shape(half_rows, 2 * COLS), shape(BLOCK, COLS), shape(BLOCK, COLS)],
         after=(prev_keys, top),
-    )(along_y(first, 1), along_y(rest, -1), ahead_g, behind_g)
-    last_other = along_seq(last, dc=1)
+    )(three, along_y(first, 1), along_y(rest, -1), ahead_g, behind_g)
+    mids_other = along_seq(mids_own, dc=1)
     grads = [grads, ahead_g, along_x(beyond[0], 1), along_x(beyond[1], -1), behind_g]
 
     far_own, far_other, prev_kv, attention, lse, *parts = call(
@@ -569,8 +569,8 @@
         flops=4 * pair_flops * 1536 + 2 * BLOCK * 2048 * COLS,
         count=2 * BLOCK * 1536,
     )(
-        near_window, mid_start, queries, out_weight, prev_keys, prev_values, last, three_other,
-        last_other, far_three, top, sums, out,
+        near_window, mid_start, queries, out_weight, prev_keys, prev_values, mids_own, mids_other,
+        far_three, top, sums, out,
     )
 
     attention_grad, delta, weight_own, weight_other = call(

time: 119 us -> 122 us (1.025)
  starting transfers between devices: 51.2 us -> 60.8 us
  waiting for transfers between devices: 39.4 us -> 32.1 us
    ppermute x17 -> x16, starting transfers between devices: 32.8 us -> 42.3 us  [along_seq(): return lax.ppermute(value, 'seq', pairs)]
    ppermute x17 -> x16, waiting for transfers between devices: 33.5 us -> 28.5 us  [along_seq(): return lax.ppermute(value, 'seq', pairs)]
    ppermute x10, waiting for transfers between devices: 5.82 us -> 3.56 us  [along_head(): return lax.ppermute(value, 'head', pairs)]
  transfers between devices with their start and end apart: 30 -> 29, of which waited for: 15 -> 12; matrix products, arithmetic and copies ran while one was open for 2% -> 2% of each run, Pallas kernels for 13% -> 13%
where the time goes in v2:
time: 122 us; the launch traced here: 121 us
  starting transfers between devices  60.8 us (50%)
  waiting for transfers between devices  32.1 us (26%)
  Pallas kernels  25.6 us (21%)
  local copies, waits for them, and re-layouts  2.01 us (2%)
    ppermute x16, starting transfers between devices, along_seq(): return lax.ppermute(value, 'seq', pairs)  42.3 us
    ppermute x16, waiting for transfers between devices, along_seq(): return lax.ppermute(value, 'seq', pairs)  28.5 us
    pallas_call x18, Pallas kernels, run(): pl.pallas_call(body, out_shape=list(outs), in_specs=[pl.BlockSpec(memory_...  25.6 us
    ppermute x10, starting transfers between devices, along_head(): return lax.ppermute(value, 'head', pairs)  13.3 us
    ppermute x3, starting transfers between devices, passed_along(): lax.ppermute(value, 'seq', [(source, source + steps) for source in range(...  5.18 us
    ppermute x10, waiting for transfers between devices, along_head(): return lax.ppermute(value, 'head', pairs)  3.56 us
  transfers between devices with their start and end apart: 29, of which 12 were waited for; matrix products, arithmetic and copies ran while one was open for 2% of the time, Pallas kernels for 13%

profile of v2, /device:TPU:32, one launch (start us, length us, event | category | flops | bytes accessed | tf_op | source)
XLA Modules:
  0.0 121.4 jit_solution(13156043561647282200)
XLA Ops:
  4.8 4.6 %collective-permute-start.2 = (bf16[64,512]{1,0:T(8,128)(2,1)S(1)}, bf16[64,512]{1,0:T(8,128)(2,1)S(1)}, u32[]{:S(2)}, u32[]{:S(2)}) collective-permute-start(bf16[64,512]{1,0:T(8,128)(2,1)S(1)} %shard_map.110.refs_0_), channel_id=1, source_target_pairs={{0,192},{8,200},{16,208},{24,216},{32,224},{40,232},{48,240},{56,2... | collective-permute-start | bytes 196616 | tf_op jit(solution)/shard_map/ppermute | solution.py:41
  10.4 2.8 %collective-permute-start = (bf16[64,512]{1,0:T(8,128)(2,1)S(1)}, bf16[64,512]{1,0:T(8,128)(2,1)S(1)}, u32[]{:S(2)}, u32[]{:S(2)}) collective-permute-start(bf16[64,512]{1,0:T(8,128)(2,1)S(1)} %shard_map.110.refs_0_), channel_id=1, source_target_pairs={{0,64},{8,72},{16,80},{24,88},{32,96},{40,104},{48,112},{56,120},{... | collective-permute-start | bytes 196616 | tf_op jit(solution)/shard_map/ppermute | solution.py:41
  13.5 5.6 %collective-permute-done.1.refs_2_ = bf16[64,512]{1,0:T(8,128)(2,1)S(1)} collective-permute-done((bf16[64,512]{1,0:T(8,128)(2,1)S(1)}, bf16[64,512]{1,0:T(8,128)(2,1)S(1)}, u32[]{:S(2)}, u32[]{:S(2)}) %collective-permute-start.1) | collective-permute-done | bytes 65568 | tf_op jit(solution)/shard_map/ppermute | solution.py:41
  19.4 3.1 %collective-permute-start.5 = (bf16[256,512]{1,0:T(8,128)(2,1)S(1)}, bf16[256,512]{1,0:T(8,128)(2,1)S(1)}, u32[]{:S(2)}, u32[]{:S(2)}) collective-permute-start(bf16[256,512]{1,0:T(8,128)(2,1)S(1)} %get-tuple-element.58.refs_0_), channel_id=1, source_target_pairs={{0,48},{8,56},{16,0},{24,8},{32,16},{40,24},{48,32},{56,40},{64,11... | collective-permute-start | bytes 786440 | tf_op jit(solution)/shard_map/ppermute | solution.py:41
  22.5 2.8 %collective-permute-start.11 = (bf16[1024,256]{1,0:T(8,128)(2,1)S(1)}, bf16[1024,256]{1,0:T(8,128)(2,1)S(1)}, u32[]{:S(2)}, u32[]{:S(2)}) collective-permute-start(bf16[1024,256]{1,0:T(8,128)(2,1)S(1)} %get-tuple-element.63.refs_2_), channel_id=1, source_target_pairs={{0,3},{1,0},{2,1},{3,2},{4,7},{5,4},{6,5},{7,6},{8,11},{9,8},{10,9... | collective-permute-start | bytes 1572872 | tf_op jit(solution)/shard_map/ppermute | solution.py:49
  26.4 3.7 %collective-permute-done.4.refs_1_ = bf16[256,512]{1,0:T(8,128)(2,1)S(1)} collective-permute-done((bf16[256,512]{1,0:T(8,128)(2,1)S(1)}, bf16[256,512]{1,0:T(8,128)(2,1)S(1)}, u32[]{:S(2)}, u32[]{:S(2)}) %collective-permute-start.4) | collective-permute-done | bytes 262176 | tf_op jit(solution)/shard_map/ppermute | solution.py:41
  31.6 3.2 %collective-permute-start.9 = (bf16[128,512]{1,0:T(8,128)(2,1)S(1)}, bf16[128,512]{1,0:T(8,128)(2,1)S(1)}, u32[]{:S(2)}, u32[]{:S(2)}) collective-permute-start(bf16[128,512]{1,0:T(8,128)(2,1)S(1)} %get-tuple-element.62), channel_id=1, source_target_pairs={{0,48},{8,56},{16,0},{24,8},{32,16},{40,24},{48,32},{56,40},{64,11... | collective-permute-start | bytes 393224 | tf_op jit(solution)/shard_map/ppermute | solution.py:41
  34.8 3.0 %shard_map.113 = (bf16[768,512]{1,0:T(8,128)(2,1)S(1)}, f32[2,512]{1,0:T(2,128)S(1)}, f32[2,512]{1,0:T(2,128)S(1)}, f32[256,512]{1,0:T(8,128)S(1)}) custom-call(s32[32]{0:T(128)S(1)} %copy-done.4, s32[32]{0:T(128)S(1)} %copy-done.3, bf16[512,256]{1,0:T(8,128)(2,1)S(1)} %copy-done.2, ...), custom_call_target="tpu_custom_call" | custom-call | flops 1610612736 | bytes 2892032 | tf_op jit(solution)/shard_map/pallas_call | solution.py:81
  37.9 2.5 %collective-permute-start.12 = (bf16[1024,512]{1,0:T(8,128)(2,1)S(1)}, bf16[1024,512]{1,0:T(8,128)(2,1)S(1)}, u32[]{:S(2)}, u32[]{:S(2)}) collective-permute-start(bf16[1024,512]{1,0:T(8,128)(2,1)S(1)} %get-tuple-element.65.refs_6_), channel_id=1, source_target_pairs={{0,8},{8,0},{16,24},{24,16},{32,40},{40,32},{48,56},{56,48},{64,72... | collective-permute-start | bytes 3145736 | tf_op jit(solution)/shard_map/ppermute | solution.py:41
  40.4 2.6 %collective-permute-start.7 = (bf16[512,256]{1,0:T(8,128)(2,1)S(1)}, bf16[512,256]{1,0:T(8,128)(2,1)S(1)}, u32[]{:S(2)}, u32[]{:S(2)}) collective-permute-start(bf16[512,256]{1,0:T(8,128)(2,1)S(1)} %copy-done.5), channel_id=1, source_target_pairs={{0,8},{8,16},{16,24},{24,32},{32,40},{40,48},{48,56},{56,64},{64,7... | collective-permute-start | bytes 786440 | tf_op jit(solution)/shard_map/ppermute | solution.py:67
  46.3 4.7 %shard_map.115 = (bf16[1024,512]{1,0:T(8,128)(2,1)S(1)}, bf16[1024,512]{1,0:T(8,128)(2,1)S(1)}, bf16[512,512]{1,0:T(8,128)(2,1)S(1)}, bf16[512,256]{1,0:T(8,128)...) custom-call(s32[32]{0:T(128)S(1)} %copy-done.4, ...), custom_call_target="tpu_custom_call" | custom-call | flops 2147483648 | bytes 10236160 | tf_op jit(solution)/shard_map/pallas_call | solution.py:81
  52.5 3.0 %shard_map.116 = (bf16[512,256]{1,0:T(8,128)(2,1)S(1)}, f32[2,512]{1,0:T(2,128)S(1)}, bf16[1024,256]{1,0:T(8,128)(2,1)S(1)}, bf16[1024,256]{1,0:T(8,128)(2,1)S(1)}) custom-call(bf16[256,2048]{1,0:T(8,128)(2,1)S(1)} %copy-done.1, bf16[512,256]{1,0:T(8,128)(2,1)S(1)} %get-tuple-element.75.refs_1_, bf16[1024,256]{1,0:T(8,128)(2,1)S(1)} %get-tuple-element.63.refs_2_, ...), custom_call_target="tpu_custom_call" | custom-call | flops 1073741824 | bytes 4722688 | tf_op jit(solution)/shard_map/pallas_call | solution.py:81
  57.5 3.9 %shard_map.118 = (bf16[1024,768]{1,0:T(8,128)(2,1)S(1)}, f32[256,512]{1,0:T(8,128)S(1)}) custom-call(s32[32]{0:T(128)S(1)} %copy-done.4, bf16[512,256]{1,0:T(8,128)(2,1)S(1)} %copy-done.2, bf16[1024,512]{1,0:T(8,128)(2,1)S(1)} %get-tuple-element.81.refs_2_, f32[2,512]{1,0:T(2,128)S(1)} %get-tuple-element.74.refs_3_.refs_2_, ...), custom_call_target="tpu_custom_call" | custom-call | flops 2684354560 | bytes 4726912 | tf_op jit(solution)/shard_map/pallas_call | solution.py:81
  62.8 3.1 %collective-permute-start.13 = (bf16[1024,256]{1,0:T(8,128)(2,1)S(1)}, bf16[1024,256]{1,0:T(8,128)(2,1)S(1)}, u32[]{:S(2)}, u32[]{:S(2)}) collective-permute-start(bf16[1024,256]{1,0:T(8,128)(2,1)S(1)} %get-tuple-element.70), channel_id=1, source_target_pairs={{0,3},{1,0},{2,1},{3,2},{4,7},{5,4},{6,5},{7,6},{8,11},{9,8},{10,9... | collective-permute-start | bytes 1572872 | tf_op jit(solution)/shard_map/ppermute | solution.py:49
  65.9 3.8 %shard_map.119 = (bf16[1024,768]{1,0:T(8,128)(2,1)S(1)}, f32[256,512]{1,0:T(8,128)S(1)}) custom-call(s32[32]{0:T(128)S(1)} %copy-done.4, bf16[512,256]{1,0:T(8,128)(2,1)S(1)} %copy-done.2, bf16[1024,512]{1,0:T(8,128)(2,1)S(1)} %get-tuple-element.80.refs_2_, f32[2,512]{1,0:T(2,128)S(1)} %get-tuple-element.74.refs_3_.refs_2_, ...), custom_call_target="tpu_custom_call" | custom-call | flops 2684354560 | bytes 4726912 | tf_op jit(solution)/shard_map/pallas_call | solution.py:81
  70.1 2.8 %collective-permute-start.22 = (bf16[256,768]{1,0:T(8,128)(2,1)S(1)}, bf16[256,768]{1,0:T(8,128)(2,1)S(1)}, u32[]{:S(2)}, u32[]{:S(2)}) collective-permute-start(bf16[256,768]{1,0:T(8,128)(2,1)S(1)} %get-tuple-element.97), channel_id=1, source_target_pairs={{0,16},{8,24},{16,32},{24,40},{32,48},{40,56},{48,0},{56,8},{64,80... | collective-permute-start | bytes 1179656 | tf_op jit(solution)/shard_map/ppermute | solution.py:41
  72.9 4.8 %collective-permute-start.21 = (bf16[256,768]{1,0:T(8,128)(2,1)S(1)}, bf16[256,768]{1,0:T(8,128)(2,1)S(1)}, u32[]{:S(2)}, u32[]{:S(2)}) collective-permute-start(bf16[256,768]{1,0:T(8,128)(2,1)S(1)} %get-tuple-element.90.refs_6_), channel_id=1, source_target_pairs={{0,48},{8,56},{16,0},{24,8},{32,16},{40,24},{48,32},{56,40},{64,11... | collective-permute-start | bytes 1179656 | tf_op jit(solution)/shard_map/ppermute | solution.py:41
  84.0 3.2 %collective-permute-done.22.refs_3_.refs_2_ = bf16[256,768]{1,0:T(8,128)(2,1)S(1)} collective-permute-done((bf16[256,768]{1,0:T(8,128)(2,1)S(1)}, bf16[256,768]{1,0:T(8,128)(2,1)S(1)}, u32[]{:S(2)}, u32[]{:S(2)}) %collective-permute-start.22) | collective-permute-done | bytes 393248 | tf_op jit(solution)/shard_map/ppermute | solution.py:41
  88.5 3.4 %collective-permute-start.24 = (bf16[128,768]{1,0:T(8,128)(2,1)S(1)}, bf16[128,768]{1,0:T(8,128)(2,1)S(1)}, u32[]{:S(2)}, u32[]{:S(2)}) collective-permute-start(bf16[128,768]{1,0:T(8,128)(2,1)S(1)} %get-tuple-element.98.refs_5_), channel_id=1, source_target_pairs={{0,48},{8,56},{16,0},{24,8},{32,16},{40,24},{48,32},{56,40},{64,11... | collective-permute-start | bytes 589832 | tf_op jit(solution)/shard_map/ppermute | solution.py:41
  92.4 4.5 %collective-permute-done.25.refs_4_ = bf16[128,768]{1,0:T(8,128)(2,1)S(1)} collective-permute-done((bf16[128,768]{1,0:T(8,128)(2,1)S(1)}, bf16[128,768]{1,0:T(8,128)(2,1)S(1)}, u32[]{:S(2)}, u32[]{:S(2)}) %collective-permute-start.25) | collective-permute-done | bytes 196640 | tf_op jit(solution)/shard_map/ppermute | solution.py:41
  97.0 2.9 %collective-permute-start.26 = (bf16[64,768]{1,0:T(8,128)(2,1)S(1)}, bf16[64,768]{1,0:T(8,128)(2,1)S(1)}, u32[]{:S(2)}, u32[]{:S(2)}) collective-permute-start(bf16[64,768]{1,0:T(8,128)(2,1)S(1)} %get-tuple-element.105), channel_id=1, source_target_pairs={{0,192},{8,200},{16,208},{24,216},{32,224},{40,232},{48,240},{56,2... | collective-permute-start | bytes 294920 | tf_op jit(solution)/shard_map/ppermute | solution.py:41
  99.9 7.7 %collective-permute-start.27 = (bf16[64,768]{1,0:T(8,128)(2,1)S(1)}, bf16[64,768]{1,0:T(8,128)(2,1)S(1)}, u32[]{:S(2)}, u32[]{:S(2)}) collective-permute-start(bf16[64,768]{1,0:T(8,128)(2,1)S(1)} %get-tuple-element.106), channel_id=1, source_target_pairs={{0,128},{8,136},{16,144},{24,152},{32,160},{40,168},{48,176},{56,1... | collective-permute-start | bytes 294920 | tf_op jit(solution)/shard_map/ppermute | solution.py:41
  107.6 2.8 %collective-permute-start.28 = (bf16[64,768]{1,0:T(8,128)(2,1)S(1)}, bf16[64,768]{1,0:T(8,128)(2,1)S(1)}, u32[]{:S(2)}, u32[]{:S(2)}) collective-permute-start(bf16[64,768]{1,0:T(8,128)(2,1)S(1)} %get-tuple-element.107), channel_id=1, source_target_pairs={{0,64},{8,72},{16,80},{24,88},{32,96},{40,104},{48,112},{56,120},{... | collective-permute-start | bytes 294920 | tf_op jit(solution)/shard_map/ppermute | solution.py:41
  111.2 9.2 %collective-permute-done.27.refs_2_ = bf16[64,768]{1,0:T(8,128)(2,1)S(1)} collective-permute-done((bf16[64,768]{1,0:T(8,128)(2,1)S(1)}, bf16[64,768]{1,0:T(8,128)(2,1)S(1)}, u32[]{:S(2)}, u32[]{:S(2)}) %collective-permute-start.27) | collective-permute-done | bytes 98336 | tf_op jit(solution)/shard_map/ppermute | solution.py:41
  (66 shorter events, 26.8 us)
Async XLA Ops:
  0.6 18.7 %collective-permute-start.3 = (bf16[512,256]{1,0:T(8,128)(2,1)}, bf16[512,256]{1,0:T(8,128)(2,1)S(1)}, u32[]{:S(2)}, u32[]{:S(2)}) collective-permute-start(bf16[512,256]{1,0:T(8,128)(2,1)} %refs_4_.1), channel_id=1, source_target_pairs={{0,4},{1,5},{2,6},{3,7},{4,0},{5,1},{6,2},{7,3},{8,12},{9,13},{10,... | collective-permute-start | bytes 786440 | tf_op jit(solution)/shard_map/ppermute | solution.py:49
  4.8 8.7 %collective-permute-start.2 = (bf16[64,512]{1,0:T(8,128)(2,1)S(1)}, bf16[64,512]{1,0:T(8,128)(2,1)S(1)}, u32[]{:S(2)}, u32[]{:S(2)}) collective-permute-start(bf16[64,512]{1,0:T(8,128)(2,1)S(1)} %shard_map.110.refs_0_), channel_id=1, source_target_pairs={{0,192},{8,200},{16,208},{24,216},{32,224},{40,232},{48,240},{56,2... | collective-permute-start | bytes 196616 | tf_op jit(solution)/shard_map/ppermute | solution.py:41
  9.4 9.7 %collective-permute-start.1 = (bf16[64,512]{1,0:T(8,128)(2,1)S(1)}, bf16[64,512]{1,0:T(8,128)(2,1)S(1)}, u32[]{:S(2)}, u32[]{:S(2)}) collective-permute-start(bf16[64,512]{1,0:T(8,128)(2,1)S(1)} %shard_map.110.refs_0_), channel_id=1, source_target_pairs={{0,128},{8,136},{16,144},{24,152},{32,160},{40,168},{48,176},{56,1... | collective-permute-start | bytes 196616 | tf_op jit(solution)/shard_map/ppermute | solution.py:41
  10.4 8.9 %collective-permute-start = (bf16[64,512]{1,0:T(8,128)(2,1)S(1)}, bf16[64,512]{1,0:T(8,128)(2,1)S(1)}, u32[]{:S(2)}, u32[]{:S(2)}) collective-permute-start(bf16[64,512]{1,0:T(8,128)(2,1)S(1)} %shard_map.110.refs_0_), channel_id=1, source_target_pairs={{0,64},{8,72},{16,80},{24,88},{32,96},{40,104},{48,112},{56,120},{... | collective-permute-start | bytes 196616 | tf_op jit(solution)/shard_map/ppermute | solution.py:41
  22.5 15.3 %collective-permute-start.11 = (bf16[1024,256]{1,0:T(8,128)(2,1)S(1)}, bf16[1024,256]{1,0:T(8,128)(2,1)S(1)}, u32[]{:S(2)}, u32[]{:S(2)}) collective-permute-start(bf16[1024,256]{1,0:T(8,128)(2,1)S(1)} %get-tuple-element.63.refs_2_), channel_id=1, source_target_pairs={{0,3},{1,0},{2,1},{3,2},{4,7},{5,4},{6,5},{7,6},{8,11},{9,8},{10,9... | collective-permute-start | bytes 1572872 | tf_op jit(solution)/shard_map/ppermute | solution.py:49
  25.2 12.6 %collective-permute-start.10 = (bf16[1024,256]{1,0:T(8,128)(2,1)S(1)}, bf16[1024,256]{1,0:T(8,128)(2,1)S(1)}, u32[]{:S(2)}, u32[]{:S(2)}) collective-permute-start(bf16[1024,256]{1,0:T(8,128)(2,1)S(1)} %get-tuple-element.63.refs_2_), channel_id=1, source_target_pairs={{0,1},{1,2},{2,3},{3,0},{4,5},{5,6},{6,7},{7,4},{8,9},{9,10},{10,1... | collective-permute-start | bytes 1572872 | tf_op jit(solution)/shard_map/ppermute | solution.py:49
  30.2 7.6 %collective-permute-start.6 = (bf16[512,256]{1,0:T(8,128)(2,1)S(1)}, bf16[512,256]{1,0:T(8,128)(2,1)S(1)}, u32[]{:S(2)}, u32[]{:S(2)}) collective-permute-start(bf16[512,256]{1,0:T(8,128)(2,1)S(1)} %get-tuple-element.59), channel_id=1, source_target_pairs={{0,8},{8,16},{16,24},{24,32},{32,40},{40,48},{48,56},{56,64},{64,7... | collective-permute-start | bytes 786440 | tf_op jit(solution)/shard_map/ppermute | solution.py:67
  37.9 8.4 %collective-permute-start.12 = (bf16[1024,512]{1,0:T(8,128)(2,1)S(1)}, bf16[1024,512]{1,0:T(8,128)(2,1)S(1)}, u32[]{:S(2)}, u32[]{:S(2)}) collective-permute-start(bf16[1024,512]{1,0:T(8,128)(2,1)S(1)} %get-tuple-element.65.refs_6_), channel_id=1, source_target_pairs={{0,8},{8,0},{16,24},{24,16},{32,40},{40,32},{48,56},{56,48},{64,72... | collective-permute-start | bytes 3145736 | tf_op jit(solution)/shard_map/ppermute | solution.py:41
  43.0 9.5 %collective-permute-start.15 = (bf16[512,256]{1,0:T(8,128)(2,1)S(1)}, bf16[512,256]{1,0:T(8,128)(2,1)S(1)}, u32[]{:S(2)}, u32[]{:S(2)}) collective-permute-start(bf16[512,256]{1,0:T(8,128)(2,1)S(1)} %get-tuple-element.76), channel_id=1, source_target_pairs={{0,1},{1,2},{2,3},{3,0},{4,5},{5,6},{6,7},{7,4},{8,9},{9,10},{10,1... | collective-permute-start | bytes 786440 | tf_op jit(solution)/shard_map/ppermute | solution.py:49
  44.6 7.9 %collective-permute-start.16 = (bf16[512,256]{1,0:T(8,128)(2,1)S(1)}, bf16[512,256]{1,0:T(8,128)(2,1)S(1)}, u32[]{:S(2)}, u32[]{:S(2)}) collective-permute-start(bf16[512,256]{1,0:T(8,128)(2,1)S(1)} %get-tuple-element.77), channel_id=1, source_target_pairs={{0,3},{1,0},{2,1},{3,2},{4,7},{5,4},{6,5},{7,6},{8,11},{9,8},{10,9... | collective-permute-start | bytes 786440 | tf_op jit(solution)/shard_map/ppermute | solution.py:49
  61.4 8.4 %collective-permute-start.17 = (bf16[1024,768]{1,0:T(8,128)(2,1)S(1)}, bf16[1024,768]{1,0:T(8,128)(2,1)S(1)}, u32[]{:S(2)}, u32[]{:S(2)}) collective-permute-start(bf16[1024,768]{1,0:T(8,128)(2,1)S(1)} %get-tuple-element.89), channel_id=1, source_target_pairs={{0,8},{8,0},{16,24},{24,16},{32,40},{40,32},{48,56},{56,48},{64,72... | collective-permute-start | bytes 4718600 | tf_op jit(solution)/shard_map/ppermute | solution.py:41
  61.5 16.3 %collective-permute-start.18 = (bf16[512,512]{1,0:T(8,128)(2,1)S(1)}, bf16[512,512]{1,0:T(8,128)(2,1)S(1)}, u32[]{:S(2)}, u32[]{:S(2)}) collective-permute-start(bf16[512,512]{1,0:T(8,128)(2,1)S(1)} %get-tuple-element.91), channel_id=1, source_target_pairs={{8,0},{16,8},{24,16},{32,24},{40,32},{48,40},{56,48},{64,56},{72,6... | collective-permute-start | bytes 1572872 | tf_op jit(solution)/shard_map/ppermute | solution.py:67
  62.8 17.2 %collective-permute-start.13 = (bf16[1024,256]{1,0:T(8,128)(2,1)S(1)}, bf16[1024,256]{1,0:T(8,128)(2,1)S(1)}, u32[]{:S(2)}, u32[]{:S(2)}) collective-permute-start(bf16[1024,256]{1,0:T(8,128)(2,1)S(1)} %get-tuple-element.70), channel_id=1, source_target_pairs={{0,3},{1,0},{2,1},{3,2},{4,7},{5,4},{6,5},{7,6},{8,11},{9,8},{10,9... | collective-permute-start | bytes 1572872 | tf_op jit(solution)/shard_map/ppermute | solution.py:49
  65.9 15.9 %collective-permute-start.14 = (bf16[1024,256]{1,0:T(8,128)(2,1)S(1)}, bf16[1024,256]{1,0:T(8,128)(2,1)S(1)}, u32[]{:S(2)}, u32[]{:S(2)}) collective-permute-start(bf16[1024,256]{1,0:T(8,128)(2,1)S(1)} %get-tuple-element.71), channel_id=1, source_target_pairs={{0,1},{1,2},{2,3},{3,0},{4,5},{5,6},{6,7},{7,4},{8,9},{9,10},{10,1... | collective-permute-start | bytes 1572872 | tf_op jit(solution)/shard_map/ppermute | solution.py:49
  70.1 17.1 %collective-permute-start.22 = (bf16[256,768]{1,0:T(8,128)(2,1)S(1)}, bf16[256,768]{1,0:T(8,128)(2,1)S(1)}, u32[]{:S(2)}, u32[]{:S(2)}) collective-permute-start(bf16[256,768]{1,0:T(8,128)(2,1)S(1)} %get-tuple-element.97), channel_id=1, source_target_pairs={{0,16},{8,24},{16,32},{24,40},{32,48},{40,56},{48,0},{56,8},{64,80... | collective-permute-start | bytes 1179656 | tf_op jit(solution)/shard_map/ppermute | solution.py:41
  72.9 15.0 %collective-permute-start.21 = (bf16[256,768]{1,0:T(8,128)(2,1)S(1)}, bf16[256,768]{1,0:T(8,128)(2,1)S(1)}, u32[]{:S(2)}, u32[]{:S(2)}) collective-permute-start(bf16[256,768]{1,0:T(8,128)(2,1)S(1)} %get-tuple-element.90.refs_6_), channel_id=1, source_target_pairs={{0,48},{8,56},{16,0},{24,8},{32,16},{40,24},{48,32},{56,40},{64,11... | collective-permute-start | bytes 1179656 | tf_op jit(solution)/shard_map/ppermute | solution.py:41
  81.9 10.0 %collective-permute-start.19 = (bf16[512,256]{1,0:T(8,128)(2,1)S(1)}, bf16[512,256]{1,0:T(8,128)(2,1)S(1)}, u32[]{:S(2)}, u32[]{:S(2)}) collective-permute-start(bf16[512,256]{1,0:T(8,128)(2,1)S(1)} %get-tuple-element.93), channel_id=1, source_target_pairs={{0,3},{1,0},{2,1},{3,2},{4,7},{5,4},{6,5},{7,6},{8,11},{9,8},{10,9... | collective-permute-start | bytes 786440 | tf_op jit(solution)/shard_map/ppermute | solution.py:49
  83.4 8.8 %collective-permute-start.20 = (bf16[512,256]{1,0:T(8,128)(2,1)S(1)}, bf16[512,256]{1,0:T(8,128)(2,1)S(1)}, u32[]{:S(2)}, u32[]{:S(2)}) collective-permute-start(bf16[512,256]{1,0:T(8,128)(2,1)S(1)} %get-tuple-element.94), channel_id=1, source_target_pairs={{0,1},{1,2},{2,3},{3,0},{4,5},{5,6},{6,7},{7,4},{8,9},{9,10},{10,1... | collective-permute-start | bytes 786440 | tf_op jit(solution)/shard_map/ppermute | solution.py:49
  88.0 8.9 %collective-permute-start.25 = (bf16[128,768]{1,0:T(8,128)(2,1)S(1)}, bf16[128,768]{1,0:T(8,128)(2,1)S(1)}, u32[]{:S(2)}, u32[]{:S(2)}) collective-permute-start(bf16[128,768]{1,0:T(8,128)(2,1)S(1)} %get-tuple-element.103), channel_id=1, source_target_pairs={{0,16},{8,24},{16,32},{24,40},{32,48},{40,56},{48,0},{56,8},{64,80... | collective-permute-start | bytes 589832 | tf_op jit(solution)/shard_map/ppermute | solution.py:41
  88.5 8.4 %collective-permute-start.24 = (bf16[128,768]{1,0:T(8,128)(2,1)S(1)}, bf16[128,768]{1,0:T(8,128)(2,1)S(1)}, u32[]{:S(2)}, u32[]{:S(2)}) collective-permute-start(bf16[128,768]{1,0:T(8,128)(2,1)S(1)} %get-tuple-element.98.refs_5_), channel_id=1, source_target_pairs={{0,48},{8,56},{16,0},{24,8},{32,16},{40,24},{48,32},{56,40},{64,11... | collective-permute-start | bytes 589832 | tf_op jit(solution)/shard_map/ppermute | solution.py:41
  92.3 18.1 %collective-permute-start.23 = (bf16[512,256]{1,0:T(8,128)(2,1)S(1)}, bf16[512,256]{1,0:T(8,128)(2,1)S(1)}, u32[]{:S(2)}, u32[]{:S(2)}) collective-permute-start(bf16[512,256]{1,0:T(8,128)(2,1)S(1)} %get-tuple-element.100), channel_id=1, source_target_pairs={{0,4},{1,5},{2,6},{3,7},{4,0},{5,1},{6,2},{7,3},{8,12},{9,13},{10,... | collective-permute-start | bytes 786440 | tf_op jit(solution)/shard_map/ppermute | solution.py:49
  97.0 14.1 %collective-permute-start.26 = (bf16[64,768]{1,0:T(8,128)(2,1)S(1)}, bf16[64,768]{1,0:T(8,128)(2,1)S(1)}, u32[]{:S(2)}, u32[]{:S(2)}) collective-permute-start(bf16[64,768]{1,0:T(8,128)(2,1)S(1)} %get-tuple-element.105), channel_id=1, source_target_pairs={{0,192},{8,200},{16,208},{24,216},{32,224},{40,232},{48,240},{56,2... | collective-permute-start | bytes 294920 | tf_op jit(solution)/shard_map/ppermute | solution.py:41
  99.9 20.5 %collective-permute-start.27 = (bf16[64,768]{1,0:T(8,128)(2,1)S(1)}, bf16[64,768]{1,0:T(8,128)(2,1)S(1)}, u32[]{:S(2)}, u32[]{:S(2)}) collective-permute-start(bf16[64,768]{1,0:T(8,128)(2,1)S(1)} %get-tuple-element.106), channel_id=1, source_target_pairs={{0,128},{8,136},{16,144},{24,152},{32,160},{40,168},{48,176},{56,1... | collective-permute-start | bytes 294920 | tf_op jit(solution)/shard_map/ppermute | solution.py:41
  107.6 12.8 %collective-permute-start.28 = (bf16[64,768]{1,0:T(8,128)(2,1)S(1)}, bf16[64,768]{1,0:T(8,128)(2,1)S(1)}, u32[]{:S(2)}, u32[]{:S(2)}) collective-permute-start(bf16[64,768]{1,0:T(8,128)(2,1)S(1)} %get-tuple-element.107), channel_id=1, source_target_pairs={{0,64},{8,72},{16,80},{24,88},{32,96},{40,104},{48,112},{56,120},{... | collective-permute-start | bytes 294920 | tf_op jit(solution)/shard_map/ppermute | solution.py:41
  (11 other events, 156.6 us)
